TPU v7x, 128 devices: a whole 4x4x4 slice. The times are simulated.
128 devices in a mesh: row: 8 (over y, z_lo), col: 16 (over x, z_hi, core).
Axes of the slice: x: 4, y: 4, z: 4 (z_hi: 2, z_lo: 2; z = z_hi * 2 + z_lo), core: 2. Of those that a mesh axis runs over, the one named last changes fastest.
Arguments:
- slide_pixels: bfloat16 [3, 1024, 4096], P(None, 'row', 'col'), may hold values from -6 to 6
- stem_weight: bfloat16 [48, 96], replicated, may hold values from -0.875 to 0.875
- depth_kernel: float32 [96, 49], replicated, may hold values from -0.875 to 0.875
- expand_weight: bfloat16 [96, 384], replicated, may hold values from -0.625 to 0.625
- reduce_weight: bfloat16 [384, 96], replicated, may hold values from -0.3125 to 0.3125
- down_weight: bfloat16 [384, 192], replicated, may hold values from -0.3125 to 0.3125
- owner_weight: bfloat16 [8, 16, 192, 768], P('row', 'col'), may hold values from -0.4375 to 0.4375
- tissue_mask: int32 [16, 64], P('row', 'col'), may hold values 0 or 1
- owner_index: int32 [8, 128, 1], P('row', 'col'), may hold values from 0 to 15; in each aligned block of 8 rows (0 to 7, 8 to 15, ..., all dimensions but the last counted through in order) at most 2 rows name the same one
- patch_cotangent: bfloat16 [16, 64, 768], P('row', 'col'), may hold values from -6 to 6
Outputs:
- stem_grad: float32 [48, 96], replicated
- kernel_grad_out: float32 [96, 49], replicated
- expand_grad: float32 [96, 384], replicated
- reduce_grad: float32 [384, 96], replicated
- down_grad: float32 [384, 192], replicated
- owner_grad: float32 [8, 16, 192, 768], P('row', 'col')
Inputs may be any that keep to these rules, and one draw needn't show every extreme that they name: `owner_index`: each device's 8 patch blocks name one owner at most 2 times, a bound that some block reaches.
All inputs are finite; a program needn't handle non-finite values. No bound on the sum of `tissue_mask` on one device may be relied on, other than what follows from the above.
Results may differ from a plain program's by a relative error of at most 0.014.
Values may be sent and summed in bfloat16 or wider, within the bound.
A program may use at most 128 MiB of HBM per device.

v0:
```python
import jax
import jax.numpy as jnp
from jax import lax
from jax.sharding import PartitionSpec as P

PATCH = 64
CAP = 2


epsilon = 1e-06
slope_factor = 0.7978845608028654
cubic_factor = 0.044715


def padded_2(array, sides, width):
    for axis, dim in sides:
        count, length = (lax.axis_size(axis), array.shape[dim])
        up = [(i, (i + 1) % count) for i in range(count - 1)]
        down = [(j, i) for i, j in up]
        last = lax.slice_in_dim(array, length - width, length, axis=dim)
        leading = lax.slice_in_dim(array, 0, width, axis=dim)
        before = lax.ppermute(last, axis, up)
        after = lax.ppermute(leading, axis, down)
        array = jnp.concatenate([before, array, after], axis=dim)
    return array


def channel_norm(values, axis):
    center = values - jnp.mean(values, axis=axis, keepdims=True)
    scale = lax.rsqrt(jnp.mean(center * center, axis=axis, keepdims=True) + epsilon)
    return (center * scale, scale)


def norm_back(normed, scale, grad, axis):
    return scale * (
        grad
        - jnp.mean(grad, axis=axis, keepdims=True)
        - normed * jnp.mean(grad * normed, axis=axis, keepdims=True)
    )


def gelu_value(hidden):
    return (
        0.5
        * hidden
        * (1.0 + jnp.tanh(slope_factor * (hidden + cubic_factor * hidden * hidden * hidden)))
    )


def gelu_slope(hidden):
    tangent = jnp.tanh(slope_factor * (hidden + cubic_factor * hidden * hidden * hidden))
    return 0.5 * (1.0 + tangent) + 0.5 * hidden * (1.0 - tangent * tangent) * slope_factor * (
        1.0 + 3.0 * cubic_factor * hidden * hidden
    )


def patchify(pixels):
    channels, height, width = pixels.shape
    blocks = pixels.reshape(channels, height // 4, 4, width // 4, 4)
    return blocks.transpose(0, 2, 4, 1, 3).reshape(channels * 16, height // 4, width // 4)


def depthwise(padded, kernel, height, width):
    total = jnp.zeros((padded.shape[0], height, width), jnp.float32)
    for row_off in range(7):
        for col_off in range(7):
            tap = kernel[:, row_off * 7 + col_off][:, None, None]
            total = total + tap * padded[:, row_off : row_off + height, col_off : col_off + width]
    return total


def kernel_taps(padded, grad, height, width):
    taps = []
    for row_off in range(7):
        for col_off in range(7):
            taps.append(
                jnp.sum(
                    grad * padded[:, row_off : row_off + height, col_off : col_off + width],
                    axis=(1, 2),
                )
            )
    return jnp.stack(taps, axis=1)


def conv_back(grad_padded, kernel, height, width):
    total = jnp.zeros((grad_padded.shape[0], height, width), jnp.float32)
    for row_off in range(7):
        for col_off in range(7):
            tap = kernel[:, row_off * 7 + col_off][:, None, None]
            total = (
                total
                + tap
                * grad_padded[
                    :, 6 - row_off : 6 - row_off + height, 6 - col_off : 6 - col_off + width
                ]
            )
    return total


def owner_work(cells, cot_scaled, weight, patch_side):
    normed, scale = channel_norm(cells.astype(jnp.float32), 1)
    normed_b = normed.astype(jnp.bfloat16)
    token_pre = jnp.einsum("ke,skt->set", weight, normed_b, preferred_element_type=jnp.float32)
    pre_grad = (cot_scaled[:, :, None] / patch_side * gelu_slope(token_pre)).astype(jnp.bfloat16)
    weight_grad = jnp.einsum("skt,set->ke", normed_b, pre_grad, preferred_element_type=jnp.float32)
    normed_grad = jnp.einsum("ke,set->skt", weight, pre_grad, preferred_element_type=jnp.float32)
    cells_grad = norm_back(normed, scale, normed_grad, 1).astype(jnp.bfloat16)
    return (cells_grad, weight_grad)


def contract_cells(left, right):
    return lax.dot_general(
        left, right, (((1,), (1,)), ((), ())), preferred_element_type=jnp.float32
    )


def on_device(
    slide_pixels,
    stem_weight,
    depth_kernel,
    expand_weight,
    reduce_weight,
    down_weight,
    owner_weight,
    tissue_mask,
    owner_index,
    patch_cotangent,
):
    mesh_rows = lax.axis_size("row")
    mesh_cols = lax.axis_size("col")
    loss_scale = (mesh_rows * mesh_cols) ** (-0.5)
    patch_side = PATCH // 8
    patch_cells = patch_side * patch_side
    channels = stem_weight.shape[1]
    wide = down_weight.shape[1]
    enc_width = owner_weight.shape[3]
    pixel_blocks = patchify(slide_pixels)
    cell_h, cell_w = (pixel_blocks.shape[1], pixel_blocks.shape[2])
    flat_blocks = pixel_blocks.reshape(48, cell_h * cell_w)
    stem_pre = jnp.dot(stem_weight.T, flat_blocks, preferred_element_type=jnp.float32)
    stem_norm, stem_scale = channel_norm(stem_pre, 0)
    stem_b = stem_norm.astype(jnp.bfloat16)
    stem_out = stem_b.astype(jnp.float32)
    padded = padded_2(stem_b.reshape(channels, cell_h, cell_w), (("row", 1), ("col", 2)), 3).astype(
        jnp.float32
    )
    depth_out = depthwise(padded, depth_kernel, cell_h, cell_w).reshape(channels, cell_h * cell_w)
    mixed_norm, mixed_scale = channel_norm(depth_out, 0)
    mixed = mixed_norm.astype(jnp.bfloat16)
    hidden_pre = jnp.dot(expand_weight.T, mixed, preferred_element_type=jnp.float32)
    activated = gelu_value(hidden_pre).astype(jnp.bfloat16)
    block_out = stem_out + jnp.dot(reduce_weight.T, activated, preferred_element_type=jnp.float32)
    down_norm, down_scale = channel_norm(block_out, 0)
    down_in = down_norm.astype(jnp.bfloat16)
    down_h, down_w = (cell_h // 2, cell_w // 2)
    grouped = (
        down_in.reshape(channels, down_h, 2, down_w, 2)
        .transpose(2, 4, 0, 1, 3)
        .reshape(4 * channels, down_h * down_w)
    )
    embed = jnp.dot(down_weight.T, grouped, preferred_element_type=jnp.float32).astype(jnp.bfloat16)
    blocks_h, blocks_w = (down_h // patch_side, down_w // patch_side)
    block_count = blocks_h * blocks_w
    embed_patches = (
        embed.reshape(wide, blocks_h, patch_side, blocks_w, patch_side)
        .transpose(1, 3, 0, 2, 4)
        .reshape(block_count, wide, patch_cells)
    )
    tissue_flat = tissue_mask.reshape(block_count)
    owners = owner_index.reshape(block_count)
    cot_flat = patch_cotangent.reshape(block_count, enc_width)
    live = tissue_flat == 1
    same_dest = (owners[:, None] == owners[None, :]) & live[None, :]
    earlier = jnp.arange(block_count)[None, :] < jnp.arange(block_count)[:, None]
    slot_rank = jnp.sum((same_dest & earlier).astype(jnp.int32), axis=1)
    target = owners * CAP + slot_rank
    route = ((jnp.arange(mesh_cols * CAP)[:, None] == target[None, :]) & live[None, :]).astype(
        jnp.bfloat16
    )
    outgoing = (
        jnp.dot(
            route,
            embed_patches.reshape(block_count, wide * patch_cells),
            preferred_element_type=jnp.float32,
        )
        .astype(jnp.bfloat16)
        .reshape(mesh_cols, CAP, wide, patch_cells)
    )
    out_cot = (
        jnp.dot(route, cot_flat, preferred_element_type=jnp.float32)
        .astype(jnp.bfloat16)
        .reshape(mesh_cols, CAP, enc_width)
    )
    arrived, arrived_cot = (
        lax.all_to_all(outgoing, "col", split_axis=0, concat_axis=0, tiled=True),
        lax.all_to_all(out_cot, "col", split_axis=0, concat_axis=0, tiled=True),
    )
    slots_grad, local_grad = owner_work(
        arrived.reshape(mesh_cols * CAP, wide, patch_cells),
        arrived_cot.reshape(mesh_cols * CAP, enc_width).astype(jnp.float32) * loss_scale,
        owner_weight[0, 0],
        patch_side,
    )
    returned = lax.all_to_all(
        slots_grad.reshape(mesh_cols, CAP, wide, patch_cells),
        "col",
        split_axis=0,
        concat_axis=0,
        tiled=True,
    )
    embed_grad = (
        jnp.dot(
            route.T,
            returned.reshape(mesh_cols * CAP, wide * patch_cells),
            preferred_element_type=jnp.float32,
        )
        .astype(jnp.bfloat16)
        .reshape(block_count, wide, patch_cells)
    )
    owner_grad = local_grad[None, None]
    embed_back = (
        embed_grad.reshape(blocks_h, blocks_w, wide, patch_side, patch_side)
        .transpose(2, 0, 3, 1, 4)
        .reshape(wide, down_h * down_w)
    )
    down_grad = contract_cells(grouped, embed_back)
    group_back = jnp.dot(down_weight, embed_back, preferred_element_type=jnp.float32)
    group_back = (
        group_back.reshape(2, 2, channels, down_h, down_w)
        .transpose(2, 3, 0, 4, 1)
        .reshape(channels, cell_h * cell_w)
    )
    block_grad = norm_back(down_norm, down_scale, group_back, 0)
    out_grad = block_grad.astype(jnp.bfloat16)
    reduce_grad = contract_cells(activated, out_grad)
    act_grad = jnp.dot(reduce_weight, out_grad, preferred_element_type=jnp.float32)
    hid_grad = (act_grad * gelu_slope(hidden_pre)).astype(jnp.bfloat16)
    expand_grad = contract_cells(mixed, hid_grad)
    mixed_grad = jnp.dot(expand_weight, hid_grad, preferred_element_type=jnp.float32)
    depth_grad = norm_back(mixed_norm, mixed_scale, mixed_grad, 0).reshape(channels, cell_h, cell_w)
    kernel_grad_out = kernel_taps(padded, depth_grad, cell_h, cell_w)
    grad_padded = padded_2(depth_grad.astype(jnp.bfloat16), (("row", 1), ("col", 2)), 3).astype(
        depth_grad.dtype
    )
    conv_grad = conv_back(grad_padded, depth_kernel, cell_h, cell_w)
    stem_in_grad = block_grad + conv_grad.reshape(channels, cell_h * cell_w)
    pre_grad_stem = norm_back(stem_norm, stem_scale, stem_in_grad, 0).astype(jnp.bfloat16)
    stem_grad = contract_cells(flat_blocks, pre_grad_stem)
    stem_total, kernel_total, expand_total, reduce_total, down_total = lax.psum(
        (stem_grad, kernel_grad_out, expand_grad, reduce_grad, down_grad), ("row", "col")
    )
    return (stem_total, kernel_total, expand_total, reduce_total, down_total, owner_grad)


def solution(mesh):
    placed = (
        P(None, "row", "col"),
        P(),
        P(),
        P(),
        P(),
        P(),
        P("row", "col", None, None),
        P("row", "col"),
        P("row", "col", None),
        P("row", "col", None),
    )
    return jax.shard_map(
        on_device,
        mesh=mesh,
        in_specs=placed,
        out_specs=(P(), P(), P(), P(), P(), P("row", "col", None, None)),
        check_vma=False,
    )
```

profile of v0, /device:TPU:1, one launch (start us, length us, event | category | flops | bytes accessed | tf_op | source)
XLA Modules:
  0.0 389.4 jit_solution(14579138549200362065)
XLA Ops:
  11.1 9.1 %all-to-all-start.1 = ((bf16[16,2,768]{2,1,0:T(2,128)(2,1)}), bf16[16,2,768]{2,1,0:T(2,128)(2,1)}, u32[]{:S(2)}, u32[]{:S(2)}) async-start(bf16[16,2,768]{2,1,0:T(2,128)(2,1)} %reshape.281), calls=%async_computation.1 | async-start | bytes 98304 | tf_op jit(solution)/shard_map/all_to_all | solution.py:196
  20.2 15.3 %reshape.272 = bf16[3,32,4,64,4]{4,3,2,1,0:T(8,128)(2,1)} reshape(bf16[3,128,256]{2,1,0:T(8,128)(2,1)} %param.10) | data formatting | bytes 393216 | tf_op jit(solution)/shard_map/reshape | solution.py:59
  35.5 6.0 %copy.50 = bf16[3,4,4,32,64]{4,3,2,1,0:T(8,128)(2,1)S(1)} copy(bf16[3,4,4,32,64]{2,4,1,3,0:T(8,128)(2,1)} %bitcast.333) | data formatting | bytes 393216 | tf_op jit(solution)/shard_map/transpose | solution.py:60
  50.5 6.8 %collective-permute-start.2 = (bf16[96,38,3]{0,2,1:T(4,128)(2,1)S(1)}, bf16[96,38,3]{0,2,1:T(4,128)(2,1)S(1)}, u32[]{:S(2)}, u32[]{:S(2)}) collective-permute-start(bf16[96,38,3]{0,2,1:T(4,128)(2,1)S(1)} %get-tuple-element.69), channel_id=1, source_target_pairs={{0,1},{1,2},{2,3},{3,4},{4,5},{5,6},{6,7},{7,8},{8,9},{9,10},{10,1... | collective-permute-start | bytes 65672 | tf_op jit(solution)/shard_map/ppermute | solution.py:22
  59.9 4.2 %collective-permute-done.3 = bf16[96,38,3]{0,2,1:T(4,128)(2,1)S(1)} collective-permute-done((bf16[96,38,3]{0,2,1:T(4,128)(2,1)S(1)}, bf16[96,38,3]{0,2,1:T(4,128)(2,1)S(1)}, u32[]{:S(2)}, u32[]{:S(2)}) %collective-permute-start.3) | collective-permute-done | bytes 21920 | tf_op jit(solution)/shard_map/ppermute | solution.py:23
  64.4 8.2 %fusion.104 = (f32[32,64]{1,0:T(8,128)S(1)}, f32[96,32,64]{0,2,1:T(8,128)S(1)}) fusion(f32[96,38,70]{0,2,1:T(8,128)S(1)} %maximum_convert_fusion, f32[96]{0:T(128)} %get-tuple-element.122, f32[96]{0:T(128)} %get-tuple-element.123, f32[96]{0:T(128)} %get-tuple-element.76, f32[96]{0:T(128)} %get-tuple-element.77, f32[96]{0:T(128)} %get-tuple-element.78, ...), kind=kLoop, calls=%fused_computation.312 | loop fusion | flops 19265536 | bytes 39348608 | tf_op jit(solution)/shard_map/reduce_sum | solution.py:29
  88.6 7.8 %reshape_reshape.10 = bf16[8,12288]{1,0:T(8,128)(2,1)S(1)} reshape(bf16[2,4,192,8,8]{4,3,2,1,0:T(8,128)(2,1)} %copy.56) | data formatting | bytes 393216 | tf_op jit(solution)/shard_map/reshape;reshape | solution.py:183
  97.6 3.6 reshape.279
  103.8 5.3 %all-to-all-start = ((bf16[16,2,192,64]{2,3,1,0:T(8,128)(2,1)}), bf16[16,2,192,64]{2,3,1,0:T(8,128)(2,1)S(1)}, u32[]{:S(2)}, u32[]{:S(2)}) async-start(bf16[16,2,192,64]{2,3,1,0:T(8,128)(2,1)} %copy.57), calls=%async_computation | async-start | bytes 2097152 | tf_op jit(solution)/shard_map/all_to_all | solution.py:195
  112.2 14.1 %all-to-all-done = bf16[16,2,192,64]{2,3,1,0:T(8,128)(2,1)S(1)} async-done(((bf16[16,2,192,64]{2,3,1,0:T(8,128)(2,1)}), bf16[16,2,192,64]{2,3,1,0:T(8,128)(2,1)S(1)}, u32[]{:S(2)}, u32[]{:S(2)}) %all-to-all-start) | async-done | bytes 786464 | tf_op jit(solution)/shard_map/all_to_all | solution.py:195
  128.1 4.3 %fusion.6 = bf16[32,768,64]{1,2,0:T(8,128)(2,1)S(1)} fusion(f32[32,768]{1,0:T(8,128)S(1)} %copy-done.33, bf16[32,192,64]{1,2,0:T(8,128)(2,1)S(1)} %bitcast.345, bf16[1,1,192,768]{3,2,1,0:T(8,128)(2,1)S(1)} %copy-done), kind=kOutput, calls=%fused_computation.10 | convolution fusion | flops 633864192 | bytes 4325376 | tf_op jit(solution)/shard_map/ke,skt->set/dot_general | solution.py:103
  136.9 4.3 %all-to-all-start.2 = ((bf16[16,2,192,64]{2,3,1,0:T(8,128)(2,1)}), bf16[16,2,192,64]{2,3,1,0:T(8,128)(2,1)S(1)}, u32[]{:S(2)}, u32[]{:S(2)}) async-start(bf16[16,2,192,64]{2,3,1,0:T(8,128)(2,1)} %bitcast.341), calls=%async_computation.2 | async-start | bytes 2097152 | tf_op jit(solution)/shard_map/all_to_all | solution.py:204
  141.2 4.2 %convolution_bitcast_fusion.2 = f32[1,1,192,768]{3,2,1,0:T(8,128)} fusion(bf16[32,768,64]{1,2,0:T(8,128)(2,1)} %copy-done.16, f32[32,192,64]{1,2,0:T(8,128)} %copy-done.8), kind=kOutput, calls=%fused_computation.40 | convolution fusion | flops 604372992 | bytes 5308416 | tf_op jit(solution)/shard_map/skt,set->ke/dot_general | solution.py:105
  145.4 13.1 %all-to-all-done.2 = bf16[16,2,192,64]{2,3,1,0:T(8,128)(2,1)S(1)} async-done(((bf16[16,2,192,64]{2,3,1,0:T(8,128)(2,1)}), bf16[16,2,192,64]{2,3,1,0:T(8,128)(2,1)S(1)}, u32[]{:S(2)}, u32[]{:S(2)}) %all-to-all-start.2) | async-done | bytes 786464 | tf_op jit(solution)/shard_map/all_to_all | solution.py:204
  163.8 5.6 %reshape_reshape.11 = bf16[2,4,192,8,8]{4,3,2,1,0:T(8,128)(2,1)} reshape(bf16[8,12288]{1,0:T(8,128)(2,1)S(1)} %convolution_convert_fusion.1) | data formatting | bytes 393216 | tf_op jit(solution)/shard_map/reshape;reshape | solution.py:222
  169.4 3.8 copy.59
  206.0 3.6 multiply_reduce_fusion.19
  209.6 3.7 multiply_reduce_fusion.1
  213.8 4.5 %collective-permute-start.4 = (bf16[96,3,64]{0,2,1:T(8,128)(2,1)S(1)}, bf16[96,3,64]{0,2,1:T(8,128)(2,1)S(1)}, u32[]{:S(2)}, u32[]{:S(2)}) collective-permute-start(bf16[96,3,64]{0,2,1:T(8,128)(2,1)S(1)} %get-tuple-element.71), channel_id=1, source_target_pairs={{0,16},{16,32},{32,48},{48,64},{64,80},{80,96},{96,112},{1,17},{17... | collective-permute-start | bytes 110600 | tf_op jit(solution)/shard_map/ppermute | solution.py:22
  223.2 4.8 %collective-permute-start.6 = (bf16[96,38,3]{0,2,1:T(4,128)(2,1)S(1)}, bf16[96,38,3]{0,2,1:T(4,128)(2,1)S(1)}, u32[]{:S(2)}, u32[]{:S(2)}) collective-permute-start(bf16[96,38,3]{0,2,1:T(4,128)(2,1)S(1)} %get-tuple-element.67), channel_id=1, source_target_pairs={{0,1},{1,2},{2,3},{3,4},{4,5},{5,6},{6,7},{7,8},{8,9},{9,10},{10,1... | collective-permute-start | bytes 65672 | tf_op jit(solution)/shard_map/ppermute | solution.py:22
  231.4 5.6 %stack.199 = f32[96,49]{0,1:T(8,128)} concatenate(f32[96,1]{0,1:T(1,128)} %bitcast.399, f32[96,1]{0,1:T(1,128)} %bitcast.398, f32[96,1]{0,1:T(1,128)} %bitcast.397, f32[96,1]{0,1:T(1,128)} %bitcast.396, f32[96,1]{0,1:T(1,128)} %bitcast.395, f32[96,1]{0,1:T(1,128)} %bitcast.394, f32[96,1]{0,1:T(1,128)} %bitcast.393, f32[96,1]{0,1:T(1,128)} %bitcast.392, f32[96,1]{0,1:T(1,128)} %bitcast.391, ...), dimensions={1} | concatenate | bytes 37632 | tf_op jit(solution)/shard_map/stack | solution.py:82
  238.3 8.0 %fusion.23 = f32[96,32,64]{0,2,1:T(8,128)S(1)} fusion(f32[96,38,70]{0,2,1:T(8,128)S(1)} %maximum_convert_fusion.1, f32[96]{0:T(128)} %get-tuple-element.122, f32[96]{0:T(128)} %get-tuple-element.123, f32[96]{0:T(128)} %get-tuple-element.76, f32[96]{0:T(128)} %get-tuple-element.77, f32[96]{0:T(128)} %get-tuple-element.78, f32[96]{0:T(128)} %get-tuple-element.79, ...), kind=kLoop, calls=%fused_computation.46 | loop fusion | flops 19070976 | bytes 39340416 | tf_op jit(solution)/shard_map/add | solution.py:91
  248.3 65.5 %all-reduce = (f32[48,96]{1,0:T(8,128)}, f32[96,49]{0,1:T(8,128)}) all-reduce(f32[48,96]{1,0:T(8,128)S(1)} %convolution_bitcast_fusion.3, f32[96,49]{0,1:T(8,128)S(1)} %copy-done.32), channel_id=1, replica_groups=mesh['row'=8,'col'=16] {'row','col'}, use_global_device_ids=true, to_apply=%region_17.0 | all-reduce | flops 9312 | bytes 74496 | tf_op jit(solution)/shard_map/psum | solution.py:249
  313.8 63.7 %all-reduce.4.cloned.1.call-done = (f32[96,384]{1,0:T(8,128)}, f32[384,96]{0,1:T(8,128)}, f32[384,192]{0,1:T(8,128)}) async-done(((f32[96,384]{1,0:T(8,128)}, f32[384,96]{0,1:T(8,128)}, f32[384,192]{0,1:T(8,128)}), (f32[96,384]{1,0:T(8,128)}, f32[384,96]{0,1:T(8,128)}, f32[384,192]{0,1:T(8,128)})) %all-reduce.4.cloned.1.call-update) | async-done | bytes 589840 | tf_op jit(solution)/shard_map/psum | solution.py:249
  (258 shorter events, 98.8 us)
Async XLA Ops:
  7.2 120.9 %copy-start = (bf16[1,1,192,768]{3,2,1,0:T(8,128)(2,1)S(1)}, bf16[1,1,192,768]{3,2,1,0:T(8,128)(2,1)}, u32[]{:S(2)}) copy-start(bf16[1,1,192,768]{3,2,1,0:T(8,128)(2,1)} %param.16) | copy-start | bytes 884740
  8.0 27.5 %copy-start.36 = (pred[8]{0:T(512)(128)(4,1)}, pred[8]{0:T(512)(128)(4,1)S(1)}, u32[]{:S(2)}) copy-start(pred[8]{0:T(512)(128)(4,1)S(1)} %eq.41) | copy-start | bytes 28
  9.6 25.9 %copy-start.38 = (s32[8]{0:T(128)}, s32[8]{0:T(128)S(1)}, u32[]{:S(2)}) copy-start(s32[8]{0:T(128)S(1)} %multiply_add_fusion.3) | copy-start | bytes 100
  11.1 92.7 %all-to-all-start.1 = ((bf16[16,2,768]{2,1,0:T(2,128)(2,1)}), bf16[16,2,768]{2,1,0:T(2,128)(2,1)}, u32[]{:S(2)}, u32[]{:S(2)}) async-start(bf16[16,2,768]{2,1,0:T(2,128)(2,1)} %reshape.281), calls=%async_computation.1 | async-start | bytes 98304 | tf_op jit(solution)/shard_map/all_to_all | solution.py:196
  41.9 18.0 %copy-start.20 = (bf16[48,2048]{1,0:T(8,128)(2,1)}, bf16[48,2048]{1,0:T(8,128)(2,1)S(1)}, u32[]{:S(2)}) copy-start(bf16[48,2048]{1,0:T(8,128)(2,1)S(1)} %reshape_reshape.9) | copy-start | bytes 589828
  42.7 5.3 %collective-permute-start = (bf16[96,3,64]{0,2,1:T(8,128)(2,1)S(1)}, bf16[96,3,64]{0,2,1:T(8,128)(2,1)S(1)}, u32[]{:S(2)}, u32[]{:S(2)}) collective-permute-start(bf16[96,3,64]{0,2,1:T(8,128)(2,1)S(1)} %get-tuple-element.73), channel_id=1, source_target_pairs={{0,16},{16,32},{32,48},{48,64},{64,80},{80,96},{96,112},{1,17},{17... | collective-permute-start | bytes 110600 | tf_op jit(solution)/shard_map/ppermute | solution.py:22
  45.4 5.1 %collective-permute-start.1 = (bf16[96,3,64]{0,2,1:T(8,128)(2,1)S(1)}, bf16[96,3,64]{0,2,1:T(8,128)(2,1)S(1)}, u32[]{:S(2)}, u32[]{:S(2)}) collective-permute-start(bf16[96,3,64]{0,2,1:T(8,128)(2,1)S(1)} %get-tuple-element.74), channel_id=1, source_target_pairs={{16,0},{32,16},{48,32},{64,48},{80,64},{96,80},{112,96},{17,1},{33... | collective-permute-start | bytes 110600 | tf_op jit(solution)/shard_map/ppermute | solution.py:23
  50.5 9.4 %collective-permute-start.2 = (bf16[96,38,3]{0,2,1:T(4,128)(2,1)S(1)}, bf16[96,38,3]{0,2,1:T(4,128)(2,1)S(1)}, u32[]{:S(2)}, u32[]{:S(2)}) collective-permute-start(bf16[96,38,3]{0,2,1:T(4,128)(2,1)S(1)} %get-tuple-element.69), channel_id=1, source_target_pairs={{0,1},{1,2},{2,3},{3,4},{4,5},{5,6},{6,7},{7,8},{8,9},{9,10},{10,1... | collective-permute-start | bytes 65672 | tf_op jit(solution)/shard_map/ppermute | solution.py:22
  57.3 6.8 %collective-permute-start.3 = (bf16[96,38,3]{0,2,1:T(4,128)(2,1)S(1)}, bf16[96,38,3]{0,2,1:T(4,128)(2,1)S(1)}, u32[]{:S(2)}, u32[]{:S(2)}) collective-permute-start(bf16[96,38,3]{0,2,1:T(4,128)(2,1)S(1)} %get-tuple-element.70), channel_id=1, source_target_pairs={{1,0},{2,1},{3,2},{4,3},{5,4},{6,5},{7,6},{8,7},{9,8},{10,9},{11,1... | collective-permute-start | bytes 65672 | tf_op jit(solution)/shard_map/ppermute | solution.py:23
  103.8 22.5 %all-to-all-start = ((bf16[16,2,192,64]{2,3,1,0:T(8,128)(2,1)}), bf16[16,2,192,64]{2,3,1,0:T(8,128)(2,1)S(1)}, u32[]{:S(2)}, u32[]{:S(2)}) async-start(bf16[16,2,192,64]{2,3,1,0:T(8,128)(2,1)} %copy.57), calls=%async_computation | async-start | bytes 2097152 | tf_op jit(solution)/shard_map/all_to_all | solution.py:195
  136.9 21.6 %all-to-all-start.2 = ((bf16[16,2,192,64]{2,3,1,0:T(8,128)(2,1)}), bf16[16,2,192,64]{2,3,1,0:T(8,128)(2,1)S(1)}, u32[]{:S(2)}, u32[]{:S(2)}) async-start(bf16[16,2,192,64]{2,3,1,0:T(8,128)(2,1)} %bitcast.341), calls=%async_computation.2 | async-start | bytes 2097152 | tf_op jit(solution)/shard_map/all_to_all | solution.py:204
  141.2 236.3 %all-reduce.4.cloned.1.call-start = ((), (), s32[]{:S(2)}) async-start(), calls=%async_computation.3 | async-start | bytes 1179648 | tf_op jit(solution)/shard_map/psum | solution.py:249
  213.3 17.7 %copy-start.43 = (f32[96]{0:T(128)S(1)}, f32[96]{0:T(128)}, u32[]{:S(2)}) copy-start(f32[96]{0:T(128)} %get-tuple-element.27) | copy-start | bytes 1156
  213.3 17.7 %copy-start.44 = (f32[96]{0:T(128)S(1)}, f32[96]{0:T(128)}, u32[]{:S(2)}) copy-start(f32[96]{0:T(128)} %get-tuple-element.28) | copy-start | bytes 1156
  213.3 17.7 %copy-start.45 = (f32[96]{0:T(128)S(1)}, f32[96]{0:T(128)}, u32[]{:S(2)}) copy-start(f32[96]{0:T(128)} %get-tuple-element.29) | copy-start | bytes 1156
  213.3 17.7 %copy-start.46 = (f32[96]{0:T(128)S(1)}, f32[96]{0:T(128)}, u32[]{:S(2)}) copy-start(f32[96]{0:T(128)} %get-tuple-element.30) | copy-start | bytes 1156
  213.3 17.7 %copy-start.47 = (f32[96]{0:T(128)S(1)}, f32[96]{0:T(128)}, u32[]{:S(2)}) copy-start(f32[96]{0:T(128)} %get-tuple-element.31) | copy-start | bytes 1156
  213.4 17.7 %copy-start.48 = (f32[96]{0:T(128)S(1)}, f32[96]{0:T(128)}, u32[]{:S(2)}) copy-start(f32[96]{0:T(128)} %get-tuple-element.32) | copy-start | bytes 1156
  213.4 17.7 %copy-start.49 = (f32[96]{0:T(128)S(1)}, f32[96]{0:T(128)}, u32[]{:S(2)}) copy-start(f32[96]{0:T(128)} %get-tuple-element.33) | copy-start | bytes 1156
  213.4 17.7 %copy-start.50 = (f32[96]{0:T(128)S(1)}, f32[96]{0:T(128)}, u32[]{:S(2)}) copy-start(f32[96]{0:T(128)} %get-tuple-element.34) | copy-start | bytes 1156
  213.8 6.9 %collective-permute-start.4 = (bf16[96,3,64]{0,2,1:T(8,128)(2,1)S(1)}, bf16[96,3,64]{0,2,1:T(8,128)(2,1)S(1)}, u32[]{:S(2)}, u32[]{:S(2)}) collective-permute-start(bf16[96,3,64]{0,2,1:T(8,128)(2,1)S(1)} %get-tuple-element.71), channel_id=1, source_target_pairs={{0,16},{16,32},{32,48},{48,64},{64,80},{80,96},{96,112},{1,17},{17... | collective-permute-start | bytes 110600 | tf_op jit(solution)/shard_map/ppermute | solution.py:22
  218.3 4.8 %collective-permute-start.5 = (bf16[96,3,64]{0,2,1:T(8,128)(2,1)S(1)}, bf16[96,3,64]{0,2,1:T(8,128)(2,1)S(1)}, u32[]{:S(2)}, u32[]{:S(2)}) collective-permute-start(bf16[96,3,64]{0,2,1:T(8,128)(2,1)S(1)} %get-tuple-element.72), channel_id=1, source_target_pairs={{16,0},{32,16},{48,32},{64,48},{80,64},{96,80},{112,96},{17,1},{33... | collective-permute-start | bytes 110600 | tf_op jit(solution)/shard_map/ppermute | solution.py:23
  223.2 13.8 %collective-permute-start.6 = (bf16[96,38,3]{0,2,1:T(4,128)(2,1)S(1)}, bf16[96,38,3]{0,2,1:T(4,128)(2,1)S(1)}, u32[]{:S(2)}, u32[]{:S(2)}) collective-permute-start(bf16[96,38,3]{0,2,1:T(4,128)(2,1)S(1)} %get-tuple-element.67), channel_id=1, source_target_pairs={{0,1},{1,2},{2,3},{3,4},{4,5},{5,6},{6,7},{7,8},{8,9},{9,10},{10,1... | collective-permute-start | bytes 65672 | tf_op jit(solution)/shard_map/ppermute | solution.py:22
  228.0 9.0 %collective-permute-start.7 = (bf16[96,38,3]{0,2,1:T(4,128)(2,1)S(1)}, bf16[96,38,3]{0,2,1:T(4,128)(2,1)S(1)}, u32[]{:S(2)}, u32[]{:S(2)}) collective-permute-start(bf16[96,38,3]{0,2,1:T(4,128)(2,1)S(1)} %get-tuple-element.68), channel_id=1, source_target_pairs={{1,0},{2,1},{3,2},{4,3},{5,4},{6,5},{7,6},{8,7},{9,8},{10,9},{11,1... | collective-permute-start | bytes 65672 | tf_op jit(solution)/shard_map/ppermute | solution.py:23
  (66 other events, 724.5 us)
Sparse Core Ops, SparseCore 0:
  231.1 146.3 all-reduce.3
where the time goes:
time: 395 us; the launch traced here: 389 us
  waiting for transfers between devices  100 us (25%)
  local copies, waits for them, and re-layouts  87.9 us (22%)
  blocking collectives  65.5 us (17%)
  other arithmetic  50.9 us (13%)
  starting transfers between devices  44 us (11%)
  matrix products  25.5 us (6%)
  between operations  15.6 us (4%)
    psum x1, blocking collectives, on_device(): lax.psum((stem_grad, kernel_grad_out, expand_grad, reduce_grad, down_grad...  65.5 us
    psum x1, waiting for transfers between devices, on_device(): lax.psum((stem_grad, kernel_grad_out, expand_grad, reduce_grad, down_grad...  63.7 us
    ppermute x4, starting transfers between devices, padded_2(): before = lax.ppermute(last, axis, up)  18.8 us
    reshape x1, local copies, waits for them, and re-layouts, patchify(): blocks = pixels.reshape(channels, height // 4, 4, width // 4, 4)  15.3 us
    all_to_all x1, waiting for transfers between devices, on_device(): lax.all_to_all(outgoing, 'col', split_axis=0, concat_axis=0, tiled=True)  14.1 us
    all_to_all x1, waiting for transfers between devices, on_device(): lax.all_to_all(slots_grad.reshape(mesh_cols, CAP, wide, patch_cells), 'co...  13.1 us
    reduce_sum x3, other arithmetic, kernel_taps(): jnp.sum(grad * padded[:, row_off:row_off + height, col_off:col_off + widt...  10.3 us
    unnamed x159, local copies, waits for them, and re-layouts  9.82 us
  transfers between devices with their start and end apart: 12, of which 6 were waited for; matrix products, arithmetic and copies ran while one was open for 23% of the time, Pallas kernels for 0%

commit v1 on v0

v1 whole, which is shorter than its diff:
```python
import jax
import jax.numpy as jnp
from jax import lax
from jax.experimental import pallas as pl
from jax.experimental.pallas import tpu as pltpu
from jax.sharding import PartitionSpec as P

C0, C1, HID, E = 96, 192, 384, 768
ROWS, COLS = 8, 16
BF, F32, I32 = jnp.bfloat16, jnp.float32, jnp.int32
EPS = 1e-06
SLOPE = 0.7978845608028654
CUBIC = 0.044715
MESH = pl.DeviceIdType.MESH
NEAR = ((-1, 0), (1, 0), (0, -1), (0, 1), (-1, -1), (-1, 1), (1, -1), (1, 1))

NN = (((1,), (0,)), ((), ()))
NT = (((1,), (1,)), ((), ()))
TN = (((0,), (0,)), ((), ()))


def dot(a, b, dims=NN):
    return lax.dot_general(a, b, dims, preferred_element_type=F32)


def iota(shape, dim):
    return lax.broadcasted_iota(I32, shape, dim)


def norm_lanes(x, mask):
    mean = jnp.sum(x, axis=-1, keepdims=True) * (1.0 / C0)
    center = (x - mean) * mask
    scale = lax.rsqrt(jnp.sum(center * center, axis=-1, keepdims=True) * (1.0 / C0) + EPS)
    return center * scale, scale


def norm_back_lanes(normed, scale, grad):
    mean = jnp.sum(grad, axis=-1, keepdims=True) * (1.0 / C0)
    proj = jnp.sum(grad * normed, axis=-1, keepdims=True) * (1.0 / C0)
    return scale * (grad - mean - normed * proj)


def gelu_both(h):
    sq = h * h
    t = jnp.tanh(SLOPE * h * (1.0 + CUBIC * sq))
    half = 0.5 * (1.0 + t)
    return h * half, half + 0.5 * h * (1.0 - t * t) * (SLOPE * (1.0 + 3.0 * CUBIC * sq))


def depthwise(src, kb, dst, flip):
    def body(n, carry):
        ib, jb = n // 8, n % 8
        i0 = ib * 8
        acc = [None] * 8
        for v in range(7):
            taps = []
            for u in range(7):
                tap = 7 * u + v
                taps.append(kb[48 - tap if flip else tap])
            for r in range(14):
                x = src[i0 + r + 1, pl.ds(jb * 8 + v, 8), :]
                for u in range(7):
                    i = r - u
                    if 0 <= i < 8:
                        term = taps[u] * x
                        acc[i] = term if acc[i] is None else acc[i] + term
        for i in range(8):
            dst[i0 + i, pl.ds(pl.multiple_of(jb * 8, 8), 8), :] = acc[i]
        return carry

    lax.fori_loop(0, 32, body, 0)


def kernel(
    pix, ws, dk, we, wr, wd, wo, tissue, owners, cot,
    out_stem, out_taps, out_expand, out_reduce, out_down, out_owner,
    xe, perm, permi, wblk, ws128, dkp, kb, we128, wr128, dwp, dwt,
    pad, sn, ss, ft, conv, mn, ms, mb, act, slope, dn, ds, gp, pmt,
    cots, sbuf, rbuf, rets, ret, wt, gs, dgu, dgp, hrow, hcol, hcor,
    acc_s, acc_e, acc_r,
    g1, g1r1, g1p2, g1r2, g1p3, g1a, g2, g2r1, g2p2, g2r2, g2p3, g2a,
    px_s, px_r, a_s, a_r, b_s, b_r, h_s, h_r,
    p1_s, p1_r, p2_s, p2_r, p3_s, p3_r, q1_s, q1_r, q2_s, q2_r, q3_s, q3_r,
):
    row, col = lax.axis_index("row"), lax.axis_index("col")

    def near(n):
        dr, dc = NEAR[n]
        return lax.rem(row + (dr + ROWS), ROWS), lax.rem(col + (dc + COLS), COLS)

    def col_peer(k):
        return row, lax.rem(col + k, COLS)

    def row_peer(k):
        return lax.rem(row + k, ROWS), col

    def remote(src, dst, send, recv, dev):
        return pltpu.make_async_remote_copy(
            src_ref=src, dst_ref=dst, send_sem=send, recv_sem=recv, device_id=dev, device_id_type=MESH
        )

    barrier = pltpu.get_barrier_semaphore()
    for k in range(1, COLS):
        pl.semaphore_signal(barrier, inc=1, device_id=col_peer(k), device_id_type=MESH)
    for k in range(1, ROWS):
        pl.semaphore_signal(barrier, inc=1, device_id=row_peer(k), device_id_type=MESH)
    for n in range(4, 8):
        pl.semaphore_signal(barrier, inc=1, device_id=near(n), device_id_type=MESH)
    pl.semaphore_wait(barrier, (COLS - 1) + (ROWS - 1) + 4)

    px_src = (
        pix.at[:, 0:16, :], pix.at[:, 112:128, :], pix.at[:, :, 0:128], pix.at[:, :, 128:256],
        pix.at[:, 0:16, 0:128], pix.at[:, 0:16, 128:256], pix.at[:, 112:128, 0:128], pix.at[:, 112:128, 128:256],
    )
    px_dst = (
        xe.at[:, 144:160, 128:384], xe.at[:, 0:16, 128:384], xe.at[:, 16:144, 384:512], xe.at[:, 16:144, 0:128],
        xe.at[:, 144:160, 384:512], xe.at[:, 144:160, 0:128], xe.at[:, 0:16, 384:512], xe.at[:, 0:16, 0:128],
    )
    px = [remote(px_src[n], px_dst[n], px_s.at[n], px_r.at[n], near(n)) for n in range(8)]
    for n in range(8):
        px[n].start()

    mask = (iota((1, 128), 1) < C0).astype(F32)
    xe[:, 16:144, 128:384] = pix[...]
    pr = iota((288, 512), 0)
    perm[...] = (iota((288, 512), 1) == 116 + 4 * (pr % 72) + pr // 72).astype(F32).astype(BF)
    for s in range(4):
        permi[s] = (iota((256, 64), 0) == 4 * iota((256, 64), 1) + s).astype(F32).astype(BF)
    ws128[...] = jnp.zeros_like(ws128)
    ws128[:, 0:C0] = ws[...]
    q48 = iota((48, 48), 0)
    ql = iota((48, 128), 0)
    for s in range(4):
        pick = (iota((48, 48), 1) == (q48 // 16) * 16 + (q48 % 4) * 4 + s).astype(F32).astype(BF)
        wsel = dot(pick, ws128[...])
        for i4 in range(4):
            wblk[s, :, i4 * 128 : (i4 + 1) * 128] = jnp.where((ql // 4) % 4 == i4, wsel, 0.0).astype(BF)
    dkp[...] = jnp.zeros_like(dkp)
    dkp[0:C0, 0:49] = dk[...]
    dkt = dkp[...].T
    for t in range(49):
        kb[t] = jnp.broadcast_to(dkt[t : t + 1, :], (8, 128))
    we128[...] = jnp.zeros_like(we128)
    we128[0:C0, :] = we[...]
    wr128[...] = jnp.zeros_like(wr128)
    wr128[:, 0:C0] = wr[...]
    dwp[...] = jnp.zeros_like(dwp)
    for b in range(4):
        dwp[b * 128 : b * 128 + C0, :] = wd[b * C0 : (b + 1) * C0, :]
    dwt[...] = dwp[...].astype(F32).T.astype(BF)
    wt[...] = wo[0, 0].astype(F32).T.astype(BF)

    slots = []
    for p in range(8):
        rank = 0
        for q in range(p):
            same = jnp.where(owners[0, q, 0] == owners[0, p, 0], 1, 0)
            rank = rank + same * tissue[q // 4, q % 4]
        slots.append(jnp.where(tissue[p // 4, p % 4] == 1, owners[0, p, 0] * 2 + rank, -1000))
    rr = iota((512, 128), 0)
    ll = iota((512, 128), 1)
    patch = (rr // 256) * 4 + (rr % 32) // 8
    slot_row = jnp.zeros((512, 128), I32)
    for p in range(8):
        slot_row = jnp.where(patch == p, slots[p], slot_row)
    hit = jnp.where(((rr // 32) % 8) * 8 + rr % 8 == ll % 64, slot_row - ll // 64, -2000)
    for d in range(COLS):
        pmt[:, d * 128 : (d + 1) * 128] = (hit == 2 * d).astype(F32).astype(BF)
    cots[...] = jnp.zeros_like(cots)
    cots[0:4, :] = cot[0].astype(F32)
    cots[4:8, :] = cot[1].astype(F32)
    slot_lane = jnp.full((256, 16), -1000, I32)
    for p in range(8):
        slot_lane = jnp.where(iota((256, 16), 1) == p, slots[p], slot_lane)
    ro = iota((256, 16), 0)
    rem16 = ro % 16
    want = jnp.where(rem16 < 12, 2 * (ro // 16) + rem16 // 6, -3000)
    packed = jnp.zeros((256, 128), F32)
    for b in range(6):
        choose = jnp.where(rem16 % 6 == b, want, -3000)
        packed = packed + dot(
            (slot_lane == choose).astype(F32).astype(BF), cots[:, b * 128 : (b + 1) * 128].astype(BF)
        )
    for d in range(COLS):
        sbuf[d, C1 : C1 + 16, :] = packed[d * 16 : (d + 1) * 16].astype(BF)

    for n in range(8):
        px[n].wait_recv()

    @pl.when(row == 0)
    def _():
        xe[:, 0:16, :] = jnp.zeros((3, 16, 512), BF)

    @pl.when(row == ROWS - 1)
    def _():
        xe[:, 144:160, :] = jnp.zeros((3, 16, 512), BF)

    @pl.when(col == 0)
    def _():
        xe[:, :, 0:128] = jnp.zeros((3, 160, 128), BF)

    @pl.when(col == COLS - 1)
    def _():
        xe[:, :, 384:512] = jnp.zeros((3, 160, 128), BF)

    def stem_body(g, carry):
        at = pl.ds(pl.multiple_of(g * 16, 16), 16)
        xg = jnp.concatenate([xe[0, at, :], xe[1, at, :], xe[2, at, :]], axis=0)
        turned = dot(perm[...], xg, NT)
        total = jnp.zeros((72, 512), F32)
        for s in range(4):
            total = total + dot(turned[s * 72 : (s + 1) * 72].astype(BF), wblk[s])
        for i4 in range(4):
            normed, scale = norm_lanes(total[:, i4 * 128 : (i4 + 1) * 128], mask)
            pad[4 * g + i4] = normed.astype(BF).astype(F32)
            sn[4 * g + i4] = normed
            ss[4 * g + i4] = jnp.broadcast_to(scale, (72, 128))
        return carry

    lax.fori_loop(0, 10, stem_body, 0)

    def flat_body(g, carry):
        at = pl.ds(pl.multiple_of(g * 16 + 16, 16), 16)
        xg = jnp.concatenate([xe[0, at, 128:384], xe[1, at, 128:384], xe[2, at, 128:384]], axis=0)
        for s in range(4):
            ft[g, s * 48 : (s + 1) * 48, :] = dot(xg, permi[s]).astype(BF)
        return carry

    lax.fori_loop(0, 8, flat_body, 0)

    depthwise(pad, kb, conv, False)

    def mlp_body(b, carry):
        rows4 = pl.ds(b * 4, 4)
        rows = pl.ds(pl.multiple_of(b * 256, 256), 256)
        normed, scale = norm_lanes(conv[rows4].reshape(256, 128), mask)
        mn[rows, :] = normed
        ms[rows, :] = jnp.broadcast_to(scale, (256, 128))
        mixed = normed.astype(BF)
        mb[rows, :] = mixed
        value, grad = gelu_both(dot(mixed, we128[...]))
        value = value.astype(BF)
        act[rows, :] = value
        slope[rows, :] = grad.astype(BF)
        block = jnp.concatenate([pad[b * 4 + 4 + i, 3:67, :] for i in range(4)], axis=0)
        block = block + dot(value, wr128[...])
        normed, scale = norm_lanes(block, mask)
        dn[rows4] = normed.reshape(4, 64, 128)
        ds[rows, :] = jnp.broadcast_to(scale, (256, 128))
        return carry

    lax.fori_loop(0, 8, mlp_body, 0)

    def group_body(i, carry):
        rows = pl.ds(pl.multiple_of(i * 32, 32), 32)
        for u in range(2):
            for v in range(2):
                b = 2 * u + v
                gp[rows, b * 128 : (b + 1) * 128] = dn[2 * i + u, pl.ds(v, 32, stride=2), :].astype(BF)
        return carry

    lax.fori_loop(0, 16, group_body, 0)
    embed = dot(dwt[...], gp[...], NT).astype(BF)

    for d in range(COLS):
        sbuf[d, 0:C1, :] = dot(embed, pmt[:, d * 128 : (d + 1) * 128]).astype(BF)
    outs = []
    for k in range(1, COLS):
        peer = col_peer(k)
        cp = remote(sbuf.at[peer[1]], rbuf.at[k], a_s.at[k], a_r.at[k], peer)
        cp.start()
        outs.append(cp)

    out_owner[0, 0] = jnp.zeros((C1, E), F32)
    sel = (iota((16, E), 0) == ((iota((16, E), 1) % 128) // 64) * 6 + iota((16, E), 1) // 128).astype(F32).astype(BF)
    cot_scale = (ROWS * COLS) ** (-0.5) / 8.0

    def own(load):
        cells = load(0, C1).astype(F32)
        mean = jnp.sum(cells, axis=0, keepdims=True) * (1.0 / C1)
        center = cells - mean
        scale = lax.rsqrt(jnp.sum(center * center, axis=0, keepdims=True) * (1.0 / C1) + EPS)
        normed = center * scale
        nb = normed.astype(BF)
        cott = dot(load(C1, 16), sel, TN) * cot_scale
        back = jnp.zeros((C1, 128), F32)
        for b in range(6):
            lanes = slice(b * 128, (b + 1) * 128)
            pre = dot(wt[lanes, :], nb)
            pg = (cott[:, lanes] * gelu_both(pre)[1]).astype(BF)
            out_owner[0, 0, :, lanes] += dot(nb, pg, NT)
            back = back + dot(wo[0, 0, :, lanes], pg)
        mean = jnp.sum(back, axis=0, keepdims=True) * (1.0 / C1)
        proj = jnp.sum(back * normed, axis=0, keepdims=True) * (1.0 / C1)
        return (scale * (back - mean - normed * proj)).astype(BF)

    mine = pl.ds(pl.multiple_of(col * 128, 128), 128)

    def back_copy(k):
        dev = (row, lax.rem(col - k + COLS, COLS))
        return remote(rets.at[k], ret.at[:, mine], b_s.at[k], b_r.at[k], dev)

    ret[:, mine] = own(lambda a, n: sbuf[col, a : a + n, :])

    def own_body(k, carry):
        remote(sbuf.at[k], rbuf.at[k], a_s.at[k], a_r.at[k], col_peer(k)).wait_recv()
        rets[k] = own(lambda a, n: rbuf[k, a : a + n, :])
        back_copy(k).start()
        return carry

    lax.fori_loop(1, COLS, own_body, 0)
    for k in range(1, COLS):
        outs[k - 1].wait_send()

    for k in range(1, COLS):
        back_copy(k).wait_recv()
    eg = dot(ret[...], pmt[...], NT).astype(BF)
    egt = dot(pmt[...], ret[...], NT).astype(BF)

    for b in range(4):
        lanes = slice(b * 128, (b + 1) * 128)
        part = dot(eg, gp[:, lanes]).astype(BF)
        g1[6 + 2 * b] = part[0:96]
        g1[7 + 2 * b] = part[96:192]

    gb = dot(egt, dwt[...])
    for i in range(16):
        for b in range(4):
            gs[2 * i + b // 2, pl.ds(b % 2, 32, stride=2), :] = gb[i * 32 : (i + 1) * 32, b * 128 : (b + 1) * 128]

    acc_e[...] = jnp.zeros_like(acc_e)
    acc_r[...] = jnp.zeros_like(acc_r)

    def back_body(b, carry):
        rows4 = pl.ds(b * 4, 4)
        rows = pl.ds(pl.multiple_of(b * 256, 256), 256)
        grad = gs[rows4].reshape(256, 128)
        grad = norm_back_lanes(dn[rows4].reshape(256, 128), ds[rows, :], grad) * mask
        gs[rows4] = grad.reshape(4, 64, 128)
        og = grad.astype(BF)
        acc_r[...] += dot(og, act[rows, :], TN)
        hid = (dot(og, wr128[...], NT) * slope[rows, :].astype(F32)).astype(BF)
        acc_e[...] += dot(mb[rows, :], hid, TN)
        mg = dot(hid, we128[...], NT)
        dg = norm_back_lanes(mn[rows, :], ms[rows, :], mg) * mask
        dgu[rows4] = dg.reshape(4, 64, 128)
        return carry

    lax.fori_loop(0, 8, back_body, 0)

    h_src = (
        dgu.at[0:3], dgu.at[29:32], dgu.at[:, 0:8, :], dgu.at[:, 56:64, :],
        dgu.at[0:3, 0:8, :], dgu.at[0:3, 56:64, :], dgu.at[29:32, 0:8, :], dgu.at[29:32, 56:64, :],
    )
    h_dst = (
        hrow.at[1], hrow.at[0], hcol.at[1], hcol.at[0], hcor.at[3], hcor.at[2], hcor.at[1], hcor.at[0],
    )
    halo = [remote(h_src[n], h_dst[n], h_s.at[n], h_r.at[n], near(n)) for n in range(8)]
    for n in range(8):
        halo[n].start()

    for b in range(3):
        lanes = slice(b * 128, (b + 1) * 128)
        g1[b] = acc_e[0:C0, lanes].astype(BF)
        g1[3 + b] = acc_r[0:C0, lanes].astype(BF)
    g1[14] = jnp.zeros((96, 128), BF)
    g1[15] = jnp.zeros((96, 128), BF)

    def make_sum(g, r1, p2, r2, p3, ga, s1, t1, s2, t2, s3, t3):
        first = [
            remote(g.at[col_peer(k)[1]], r1.at[k], s1.at[k], t1.at[k], col_peer(k)) for k in range(1, COLS)
        ]
        second = [remote(p2, r2.at[row], s2.at[k], t2.at[k], row_peer(k)) for k in range(1, ROWS)]
        third = [remote(p3, ga.at[col], s3.at[k], t3.at[k], col_peer(k)) for k in range(1, COLS)]

        def start():
            for cp in first:
                cp.start()

        def turn():
            for cp in first:
                cp.wait_recv()
            total = g[col].astype(F32)
            for k in range(1, COLS):
                total = total + r1[k].astype(F32)
            p2[...] = total.astype(p2.dtype)
            r2[row] = total.astype(p2.dtype)
            for cp in second:
                cp.start()

        def spread():
            for cp in second:
                cp.wait_recv()
            total = r2[0].astype(F32)
            for k in range(1, ROWS):
                total = total + r2[k].astype(F32)
            p3[...] = total.astype(p3.dtype)
            ga[col] = total.astype(p3.dtype)
            for cp in third:
                cp.start()

        def finish():
            for cp in third:
                cp.wait_recv()

        def drain():
            for cp in first + second + third:
                cp.wait_send()

        return start, turn, spread, finish, drain

    start1, turn1, spread1, finish1, drain1 = make_sum(
        g1, g1r1, g1p2, g1r2, g1p3, g1a, p1_s, p1_r, p2_s, p2_r, p3_s, p3_r
    )
    start2, turn2, spread2, finish2, drain2 = make_sum(
        g2, g2r1, g2p2, g2r2, g2p3, g2a, q1_s, q1_r, q2_s, q2_r, q3_s, q3_r
    )
    start1()

    g2[...] = jnp.zeros_like(g2)
    for v in range(7):

        def taps_body(jb, acc, v=v):
            acc = list(acc)
            here = pl.ds(pl.multiple_of(jb * 8, 8), 8)
            grads = {}
            for r in range(38):
                x = pad[r + 1, pl.ds(jb * 8 + v, 8), :]
                if r < 32:
                    grads[r] = dgu[r, here, :]
                for u in range(7):
                    if 0 <= r - u < 32:
                        acc[u] = acc[u] + grads[r - u] * x
            return tuple(acc)

        sums = lax.fori_loop(0, 8, taps_body, tuple(jnp.zeros((8, 128), F32) for _ in range(7)))
        for u in range(7):
            at = 48 + 7 * u + v
            g2[at // 8, at % 8 : at % 8 + 1, :] = jnp.sum(sums[u], axis=0, keepdims=True)

    turn1()

    dgp[...] = jnp.zeros_like(dgp)
    for i in range(32):
        dgp[4 + i, 3:67, :] = dgu[i]
    for n in range(8):
        halo[n].wait_recv()
    top, bottom = jnp.where(row > 0, 1.0, 0.0), jnp.where(row < ROWS - 1, 1.0, 0.0)
    left, right = jnp.where(col > 0, 1.0, 0.0), jnp.where(col < COLS - 1, 1.0, 0.0)
    for i in range(3):
        dgp[1 + i, 3:67, :] = hrow[0, i] * top
        dgp[36 + i, 3:67, :] = hrow[1, i] * bottom
        dgp[1 + i, 0:3, :] = hcor[0, i, 5:8] * (top * left)
        dgp[1 + i, 67:70, :] = hcor[1, i, 0:3] * (top * right)
        dgp[36 + i, 0:3, :] = hcor[2, i, 5:8] * (bottom * left)
        dgp[36 + i, 67:70, :] = hcor[3, i, 0:3] * (bottom * right)
    dgp[4:36, 0:3, :] = hcol[0, :, 5:8, :] * left
    dgp[4:36, 67:70, :] = hcol[1, :, 0:3, :] * right

    depthwise(dgp, kb, conv, True)
    spread1()

    acc_s[...] = jnp.zeros_like(acc_s)

    def stem_back(g, carry):
        parts = []
        for i in range(4):
            grad = gs[4 * g + i] + conv[4 * g + i]
            parts.append(
                norm_back_lanes(sn[4 * g + 4 + i, 3:67, :], ss[4 * g + 4 + i, 3:67, :], grad).astype(BF)
            )
        grads = jnp.concatenate(parts, axis=1)
        for s in range(4):
            acc_s[s * 48 : (s + 1) * 48, :] += dot(ft[g, s * 48 : (s + 1) * 48, :], grads)
        return carry

    lax.fori_loop(0, 8, stem_back, 0)
    rows = iota((192, 128), 0)
    folded = jnp.zeros((192, 128), F32)
    for i4 in range(4):
        folded = folded + jnp.where((rows // 4) % 4 == i4, acc_s[:, i4 * 128 : (i4 + 1) * 128], 0.0)
    m48, q192 = iota((48, 192), 0), iota((48, 192), 1)
    rem = q192 % 48
    gather = (m48 == (rem // 16) * 16 + (rem % 4) * 4 + q192 // 48).astype(F32)
    stem = lax.dot_general(gather, folded, NN, precision=lax.Precision.HIGHEST, preferred_element_type=F32)
    for n in range(6):
        g2[n] = stem[n * 8 : (n + 1) * 8]

    start2()
    finish1()
    for b in range(3):
        lanes = slice(b * 128, (b + 1) * 128)
        out_expand[:, lanes] = g1a[b].astype(F32)
        out_reduce[lanes, :] = g1a[3 + b].astype(F32).T
    for b in range(4):
        out_down[b * C0 : (b + 1) * C0, 0:96] = g1a[6 + 2 * b].astype(F32).T[0:C0, :]
        out_down[b * C0 : (b + 1) * C0, 96:192] = g1a[7 + 2 * b].astype(F32).T[0:C0, :]
    turn2()
    spread2()
    finish2()
    for n in range(6):
        out_stem[n * 8 : (n + 1) * 8, :] = g2a[n, :, 0:C0]
    for n in range(6, 16):
        dkp[(n - 6) * 8 : (n - 5) * 8, :] = g2a[n]
    out_taps[...] = dkp[...].T[0:C0, 0:49]

    for n in range(8):
        px[n].wait_send()
        halo[n].wait_send()
    for k in range(1, COLS):
        back_copy(k).wait_send()
    drain1()
    drain2()


def on_device(pixels, ws, dk, we, wr, wd, wo, tissue, owners, cot):
    vmem = pl.BlockSpec(memory_space=pltpu.VMEM)
    smem = pl.BlockSpec(memory_space=pltpu.SMEM)
    dma = pltpu.SemaphoreType.DMA
    V = pltpu.VMEM
    outs = ((48, C0), (C0, 49), (C0, HID), (HID, C0), (4 * C0, C1), (1, 1, C1, E))
    return pl.pallas_call(
        kernel,
        out_shape=tuple(jax.ShapeDtypeStruct(s, F32) for s in outs),
        in_specs=[vmem] * 7 + [smem, smem, vmem],
        out_specs=(vmem,) * 6,
        scratch_shapes=[
            V((3, 160, 512), BF), V((288, 512), BF), V((4, 256, 64), BF), V((4, 48, 512), BF), V((48, 128), BF),
            V((128, 128), F32), V((49, 8, 128), F32), V((128, HID), BF), V((HID, 128), BF),
            V((512, C1), BF), V((C1, 512), BF),
            V((40, 72, 128), F32), V((40, 72, 128), F32), V((40, 72, 128), F32), V((8, 192, 64), BF),
            V((32, 64, 128), F32), V((2048, 128), F32), V((2048, 128), F32), V((2048, 128), BF),
            V((2048, HID), BF), V((2048, HID), BF), V((32, 64, 128), F32), V((2048, 128), F32),
            V((512, 512), BF), V((512, 2048), BF),
            V((16, E), F32), V((16, 208, 128), BF), V((16, 208, 128), BF), V((16, C1, 128), BF), V((C1, 2048), BF),
            V((E, C1), BF), V((32, 64, 128), F32), V((32, 64, 128), F32), V((40, 72, 128), F32),
            V((2, 3, 64, 128), F32), V((2, 32, 8, 128), F32), V((4, 3, 8, 128), F32),
            V((192, 512), F32), V((128, HID), F32), V((128, HID), F32),
            V((16, 96, 128), BF), V((16, 96, 128), BF), V((96, 128), BF), V((8, 96, 128), BF), V((96, 128), BF),
            V((16, 96, 128), BF),
            V((16, 8, 128), F32), V((16, 8, 128), F32), V((8, 128), F32), V((8, 8, 128), F32), V((8, 128), F32),
            V((16, 8, 128), F32),
            dma((8,)), dma((8,)), dma((16,)), dma((16,)), dma((16,)), dma((16,)), dma((8,)), dma((8,)),
            dma((16,)), dma((16,)), dma((8,)), dma((8,)), dma((16,)), dma((16,)),
            dma((16,)), dma((16,)), dma((8,)), dma((8,)), dma((16,)), dma((16,)),
        ],
        compiler_params=pltpu.CompilerParams(
            collective_id=0, has_side_effects=True, vmem_limit_bytes=56 * 1024 * 1024
        ),
    )(pixels, ws, dk, we, wr, wd, wo, tissue, owners, cot)


def solution(mesh):
    placed = (
        P(None, "row", "col"), P(), P(), P(), P(), P(), P("row", "col", None, None),
        P("row", "col"), P("row", "col", None), P("row", "col", None),
    )
    return jax.shard_map(
        on_device,
        mesh=mesh,
        in_specs=placed,
        out_specs=(P(), P(), P(), P(), P(), P("row", "col", None, None)),
        check_vma=False,
    )
```

time: 395 us -> 124 us (0.31); the launches traced: 389 us -> 124 us
  Pallas kernels: 0 us -> 112 us
  waiting for transfers between devices: 100 us -> 0 us
  local copies, waits for them, and re-layouts: 87.9 us -> 11.5 us
  blocking collectives: 65.5 us -> 0 us
  other arithmetic: 50.9 us -> 0 us
  starting transfers between devices: 44 us -> 0 us
  matrix products: 25.5 us -> 0 us
  between operations: 15.6 us -> 0.66 us
    pallas_call x0 -> x1, Pallas kernels: none -> 112 us  [on_device(): pl.pallas_call(kernel, out_shape=tuple((jax.ShapeDtypeStruct(s, F32) for...]
    psum x1 -> x0, blocking collectives: 65.5 us -> none  [on_device(): lax.psum((stem_grad, kernel_grad_out, expand_grad, reduce_grad, down_grad...]
    psum x1 -> x0, waiting for transfers between devices: 63.7 us -> none  [on_device(): lax.psum((stem_grad, kernel_grad_out, expand_grad, reduce_grad, down_grad...]
    reshape x12 -> x0, local copies, waits for them, and re-layouts: 35 us -> none  [the longest x1 15.3 us: patchify(): blocks = pixels.reshape(channels, height // 4, 4, width // 4, 4)]
    reduce_sum x14 -> x0, other arithmetic: 28 us -> none  [the longest x3 10.3 us: kernel_taps(): jnp.sum(grad * padded[:, row_off:row_off + height, col_off:col_off + widt...]
    all_to_all x3 -> x0, waiting for transfers between devices: 27.2 us -> none  [the longest x1 14.1 us: on_device(): lax.all_to_all(outgoing, 'col', split_axis=0, concat_axis=0, tiled=True)]
    dot_general x17 -> x0, matrix products: 25.5 us -> none  [the longest x1 4.34 us: owner_work(): jnp.einsum('ke,skt->set', weight, normed_b, preferred_element_type=jnp.fl...]
    ppermute x8 -> x0, starting transfers between devices: 25.2 us -> none  [the longest x4 18.8 us: padded_2(): before = lax.ppermute(last, axis, up)]
  transfers between devices with their start and end apart: 12 -> 0, of which waited for: 6 -> 0; matrix products, arithmetic and copies ran while one was open for 23% -> 0% of each run, Pallas kernels for 0% -> 0%
where the time goes in v1:
time: 124 us
  Pallas kernels  112 us (90%)
  local copies, waits for them, and re-layouts  11.5 us (9%)
    pallas_call x1, Pallas kernels, on_device(): pl.pallas_call(kernel, out_shape=tuple((jax.ShapeDtypeStruct(s, F32) for...  112 us
    unnamed x17, local copies, waits for them, and re-layouts  7.37 us
    pallas_call x3, local copies, waits for them, and re-layouts, on_device(): pl.pallas_call(kernel, out_shape=tuple((jax.ShapeDtypeStruct(s, F32) for...  4.13 us

profile of v1, /device:TPU:1, one launch (start us, length us, event | category | flops | bytes accessed | tf_op | source)
XLA Modules:
  0.0 123.9 jit_solution(2210258923207531600)
XLA Ops:
  0.6 0.0 copy-start.3
  0.6 1.4 %copy.19.owners = s32[1,8,1]{2,1,0:T(8,128)} copy(s32[1,8,1]{1,2,0:T(1,128)} %param.18) | data formatting | bytes 64 | tf_op args[8]
  2.0 1.5 %copy.16.dk = f32[96,49]{1,0:T(8,128)} copy(f32[96,49]{0,1:T(8,128)} %param.12) | data formatting | bytes 37632 | tf_op args[2]
  3.5 1.6 %copy.17.wr = bf16[384,96]{1,0:T(8,128)(2,1)} copy(bf16[384,96]{0,1:T(8,128)(2,1)} %param.14) | data formatting | bytes 147456 | tf_op args[4]
  5.1 0.0 copy-done.3
  5.1 0.8 copy.18.wd
  5.9 111.7 %shard_map.145 = (f32[48,96]{1,0:T(8,128)}, f32[96,49]{1,0:T(8,128)}, f32[96,384]{1,0:T(8,128)}, f32[384,96]{1,0:T(8,128)}, f32[384,192]{1,0:T(8,128)}, /*index=5*/f32[1,1,192,768]{3,2,1,0:T(8,128)}) custom-call(bf16[3,128,256]{2,1,0:T(8,128)(2,1)} %pix.1, bf16[48,96]{1,0:T(8,128)(2,1)} %ws.1, f32[96,49]{1,0:T(8,128)} %copy.16.dk, bf16[96,384]{1,0:T(8,128)(2,1)} %we.1, ...), custom_call_target="tpu_custom_call" | custom-call | tf_op jit(solution)/shard_map/pallas_call | solution.py:522
  117.6 0.0 copy-start.1
  117.6 1.5 %copy.20 = f32[96,49]{0,1:T(8,128)} copy(f32[96,49]{1,0:T(8,128)} %get-tuple-element.7) | data formatting | bytes 37632 | tf_op jit(solution)/shard_map/pallas_call | solution.py:522
  119.2 0.0 copy-start.4
  119.2 1.7 %copy.21 = f32[384,96]{0,1:T(8,128)} copy(f32[384,96]{1,0:T(8,128)} %get-tuple-element.9) | data formatting | bytes 294912 | tf_op jit(solution)/shard_map/pallas_call | solution.py:522
  120.9 0.0 copy-done.1
  120.9 0.0 copy-start.2
  120.9 0.0 copy-start
  120.9 0.9 copy.22
  121.8 0.0 copy-done.4
  121.8 0.6 copy.26
  122.4 0.0 copy-done.2
  122.4 0.7 copy.27
  123.0 0.0 copy-done
  123.0 0.8 copy.28
Async XLA Ops:
  0.6 4.5 %copy-start.3 = (bf16[384,192]{0,1:T(8,128)(2,1)S(1)}, bf16[384,192]{0,1:T(8,128)(2,1)}, u32[]{:S(2)}) copy-start(bf16[384,192]{0,1:T(8,128)(2,1)} %param.15) | copy-start | bytes 442372
  117.6 3.3 %copy-start.1 = (f32[384,192]{1,0:T(8,128)S(1)}, f32[384,192]{1,0:T(8,128)}, u32[]{:S(2)}) copy-start(f32[384,192]{1,0:T(8,128)} %get-tuple-element.10) | copy-start | bytes 884740
  119.2 2.6 %copy-start.4 = (f32[48,96]{1,0:T(8,128)S(1)}, f32[48,96]{1,0:T(8,128)}, u32[]{:S(2)}) copy-start(f32[48,96]{1,0:T(8,128)} %get-tuple-element.18) | copy-start | bytes 55300
  120.9 1.5 %copy-start.2 = (f32[96,384]{1,0:T(8,128)S(1)}, f32[96,384]{1,0:T(8,128)}, u32[]{:S(2)}) copy-start(f32[96,384]{1,0:T(8,128)} %get-tuple-element.20) | copy-start | bytes 442372
  120.9 2.1 %copy-start = (f32[1,1,192,768]{3,2,1,0:T(8,128)S(1)}, f32[1,1,192,768]{3,2,1,0:T(8,128)}, u32[]{:S(2)}) copy-start(f32[1,1,192,768]{3,2,1,0:T(8,128)} %get-tuple-element.23) | copy-start | bytes 1769476

commit v2 on v1

--- a/solution.py
+++ b/solution.py
@@ -72,15 +72,15 @@
 
 
 def kernel(
-    pix, ws, dk, we, wr, wd, wo, tissue, owners, cot,
+    pix, ws, dkt, we, wrt, wdt, wo, tissue, owners, cot,
     out_stem, out_taps, out_expand, out_reduce, out_down, out_owner,
-    xe, perm, permi, wblk, ws128, dkp, kb, we128, wr128, dwp, dwt,
+    xe, perm, permi, wblk, ws128, kb, we128, wr128, dwt,
     pad, sn, ss, ft, conv, mn, ms, mb, act, slope, dn, ds, gp, pmt,
-    cots, sbuf, rbuf, rets, ret, wt, gs, dgu, dgp, hrow, hcol, hcor,
+    cots, sbuf, rbuf, rets, ret, nball, pgall, wt, gs, dgu, dgp, hrow, hcol, hcor,
     acc_s, acc_e, acc_r,
-    g1, g1r1, g1p2, g1r2, g1p3, g1a, g2, g2r1, g2p2, g2r2, g2p3, g2a,
+    g1, g1r1, g1p2, g1r2, g1p3, g1a, g2, g2r1, g2p2, g2r2, g2p3, g2a, kt, g3a, g3r, g3b, g3c,
     px_s, px_r, a_s, a_r, b_s, b_r, h_s, h_r,
-    p1_s, p1_r, p2_s, p2_r, p3_s, p3_r, q1_s, q1_r, q2_s, q2_r, q3_s, q3_r,
+    p1_s, p1_r, p2_s, p2_r, p3_s, p3_r, q1_s, q1_r, q2_s, q2_r, q3_s, q3_r, r1_s, r1_r, r2_s, r2_r,
 ):
     row, col = lax.axis_index("row"), lax.axis_index("col")
 
@@ -135,28 +135,25 @@
         wsel = dot(pick, ws128[...])
         for i4 in range(4):
             wblk[s, :, i4 * 128 : (i4 + 1) * 128] = jnp.where((ql // 4) % 4 == i4, wsel, 0.0).astype(BF)
-    dkp[...] = jnp.zeros_like(dkp)
-    dkp[0:C0, 0:49] = dk[...]
-    dkt = dkp[...].T
+    kb[...] = jnp.zeros_like(kb)
     for t in range(49):
-        kb[t] = jnp.broadcast_to(dkt[t : t + 1, :], (8, 128))
+        kb[t, :, 0:C0] = jnp.broadcast_to(dkt[t : t + 1, :], (8, C0))
     we128[...] = jnp.zeros_like(we128)
     we128[0:C0, :] = we[...]
     wr128[...] = jnp.zeros_like(wr128)
-    wr128[:, 0:C0] = wr[...]
-    dwp[...] = jnp.zeros_like(dwp)
+    wr128[0:C0, :] = wrt[...]
+    dwt[...] = jnp.zeros_like(dwt)
     for b in range(4):
-        dwp[b * 128 : b * 128 + C0, :] = wd[b * C0 : (b + 1) * C0, :]
-    dwt[...] = dwp[...].astype(F32).T.astype(BF)
+        dwt[:, b * 128 : b * 128 + C0] = wdt[:, b * C0 : (b + 1) * C0]
     wt[...] = wo[0, 0].astype(F32).T.astype(BF)
 
     slots = []
     for p in range(8):
         rank = 0
         for q in range(p):
-            same = jnp.where(owners[0, q, 0] == owners[0, p, 0], 1, 0)
+            same = jnp.where(owners[0, q] == owners[0, p], 1, 0)
             rank = rank + same * tissue[q // 4, q % 4]
-        slots.append(jnp.where(tissue[p // 4, p % 4] == 1, owners[0, p, 0] * 2 + rank, -1000))
+        slots.append(jnp.where(tissue[p // 4, p % 4] == 1, owners[0, p] * 2 + rank, -1000))
     rr = iota((512, 128), 0)
     ll = iota((512, 128), 1)
     patch = (rr // 256) * 4 + (rr % 32) // 8
@@ -217,7 +214,7 @@
             ss[4 * g + i4] = jnp.broadcast_to(scale, (72, 128))
         return carry
 
-    lax.fori_loop(0, 10, stem_body, 0)
+    lax.fori_loop(0, 10, stem_body, 0, unroll=10)
 
     def flat_body(g, carry):
         at = pl.ds(pl.multiple_of(g * 16 + 16, 16), 16)
@@ -226,7 +223,7 @@
             ft[g, s * 48 : (s + 1) * 48, :] = dot(xg, permi[s]).astype(BF)
         return carry
 
-    lax.fori_loop(0, 8, flat_body, 0)
+    lax.fori_loop(0, 8, flat_body, 0, unroll=8)
 
     depthwise(pad, kb, conv, False)
 
@@ -243,13 +240,13 @@
         act[rows, :] = value
         slope[rows, :] = grad.astype(BF)
         block = jnp.concatenate([pad[b * 4 + 4 + i, 3:67, :] for i in range(4)], axis=0)
-        block = block + dot(value, wr128[...])
+        block = block + dot(value, wr128[...], NT)
         normed, scale = norm_lanes(block, mask)
         dn[rows4] = normed.reshape(4, 64, 128)
         ds[rows, :] = jnp.broadcast_to(scale, (256, 128))
         return carry
 
-    lax.fori_loop(0, 8, mlp_body, 0)
+    lax.fori_loop(0, 8, mlp_body, 0, unroll=8)
 
     def group_body(i, carry):
         rows = pl.ds(pl.multiple_of(i * 32, 32), 32)
@@ -264,107 +261,67 @@
 
     for d in range(COLS):
         sbuf[d, 0:C1, :] = dot(embed, pmt[:, d * 128 : (d + 1) * 128]).astype(BF)
-    outs = []
+    def out_copy(k):
+        peer = col_peer(k)
+        lanes = slice((k % 2) * 128, (k % 2 + 1) * 128)
+        return remote(sbuf.at[peer[1]], rbuf.at[k // 2, :, lanes], a_s.at[k], a_r.at[k], peer)
+
     for k in range(1, COLS):
-        peer = col_peer(k)
-        cp = remote(sbuf.at[peer[1]], rbuf.at[k], a_s.at[k], a_r.at[k], peer)
-        cp.start()
-        outs.append(cp)
-
-    out_owner[0, 0] = jnp.zeros((C1, E), F32)
+        out_copy(k).start()
+    rbuf[0, :, 0:128] = sbuf[col]
+
     sel = (iota((16, E), 0) == ((iota((16, E), 1) % 128) // 64) * 6 + iota((16, E), 1) // 128).astype(F32).astype(BF)
     cot_scale = (ROWS * COLS) ** (-0.5) / 8.0
-
-    def own(load):
-        cells = load(0, C1).astype(F32)
+    mine = pl.ds(pl.multiple_of(col * 128, 128), 128)
+
+    def back_copy(j, half):
+        k = 2 * j + half
+        dev = (row, lax.rem(col - k + COLS, COLS))
+        lanes = slice(half * 128, (half + 1) * 128)
+        return remote(rets.at[j, :, lanes], ret.at[:, mine], b_s.at[k], b_r.at[k], dev)
+
+    def own(j):
+        cells = rbuf[j, 0:C1, :].astype(F32)
         mean = jnp.sum(cells, axis=0, keepdims=True) * (1.0 / C1)
         center = cells - mean
         scale = lax.rsqrt(jnp.sum(center * center, axis=0, keepdims=True) * (1.0 / C1) + EPS)
         normed = center * scale
         nb = normed.astype(BF)
-        cott = dot(load(C1, 16), sel, TN) * cot_scale
-        back = jnp.zeros((C1, 128), F32)
+        nball[j] = nb
+        cots_a = dot(rbuf[j, C1 : C1 + 16, 0:128], sel, TN) * cot_scale
+        cots_b = dot(rbuf[j, C1 : C1 + 16, 128:256], sel, TN) * cot_scale
         for b in range(6):
             lanes = slice(b * 128, (b + 1) * 128)
             pre = dot(wt[lanes, :], nb)
-            pg = (cott[:, lanes] * gelu_both(pre)[1]).astype(BF)
-            out_owner[0, 0, :, lanes] += dot(nb, pg, NT)
-            back = back + dot(wo[0, 0, :, lanes], pg)
+            cott = jnp.concatenate([cots_a[:, lanes], cots_b[:, lanes]], axis=1)
+            pgall[j, lanes, :] = (cott * gelu_both(pre)[1]).astype(BF)
+        back = dot(wo[0, 0], pgall[j])
         mean = jnp.sum(back, axis=0, keepdims=True) * (1.0 / C1)
         proj = jnp.sum(back * normed, axis=0, keepdims=True) * (1.0 / C1)
-        return (scale * (back - mean - normed * proj)).astype(BF)
-
-    mine = pl.ds(pl.multiple_of(col * 128, 128), 128)
-
-    def back_copy(k):
-        dev = (row, lax.rem(col - k + COLS, COLS))
-        return remote(rets.at[k], ret.at[:, mine], b_s.at[k], b_r.at[k], dev)
-
-    ret[:, mine] = own(lambda a, n: sbuf[col, a : a + n, :])
-
-    def own_body(k, carry):
-        remote(sbuf.at[k], rbuf.at[k], a_s.at[k], a_r.at[k], col_peer(k)).wait_recv()
-        rets[k] = own(lambda a, n: rbuf[k, a : a + n, :])
-        back_copy(k).start()
-        return carry
-
-    lax.fori_loop(1, COLS, own_body, 0)
+        rets[j] = (scale * (back - mean - normed * proj)).astype(BF)
+
+    out_copy(1).wait_recv()
+    own(0)
+    ret[:, mine] = rets[0, :, 0:128]
+    back_copy(0, 1).start()
+
+    def own_body(j, carry):
+        for half in range(2):
+            k = 2 * j + half
+            lanes = slice(half * 128, (half + 1) * 128)
+            remote(sbuf.at[0], rbuf.at[j, :, lanes], a_s.at[k], a_r.at[k], col_peer(k)).wait_recv()
+        own(j)
+        for half in range(2):
+            back_copy(j, half).start()
+        return carry
+
+    lax.fori_loop(1, COLS // 2, own_body, 0)
     for k in range(1, COLS):
-        outs[k - 1].wait_send()
-
+        out_copy(k).wait_send()
     for k in range(1, COLS):
-        back_copy(k).wait_recv()
+        back_copy(k // 2, k % 2).wait_recv()
     eg = dot(ret[...], pmt[...], NT).astype(BF)
     egt = dot(pmt[...], ret[...], NT).astype(BF)
-
-    for b in range(4):
-        lanes = slice(b * 128, (b + 1) * 128)
-        part = dot(eg, gp[:, lanes]).astype(BF)
-        g1[6 + 2 * b] = part[0:96]
-        g1[7 + 2 * b] = part[96:192]
-
-    gb = dot(egt, dwt[...])
-    for i in range(16):
-        for b in range(4):
-            gs[2 * i + b // 2, pl.ds(b % 2, 32, stride=2), :] = gb[i * 32 : (i + 1) * 32, b * 128 : (b + 1) * 128]
-
-    acc_e[...] = jnp.zeros_like(acc_e)
-    acc_r[...] = jnp.zeros_like(acc_r)
-
-    def back_body(b, carry):
-        rows4 = pl.ds(b * 4, 4)
-        rows = pl.ds(pl.multiple_of(b * 256, 256), 256)
-        grad = gs[rows4].reshape(256, 128)
-        grad = norm_back_lanes(dn[rows4].reshape(256, 128), ds[rows, :], grad) * mask
-        gs[rows4] = grad.reshape(4, 64, 128)
-        og = grad.astype(BF)
-        acc_r[...] += dot(og, act[rows, :], TN)
-        hid = (dot(og, wr128[...], NT) * slope[rows, :].astype(F32)).astype(BF)
-        acc_e[...] += dot(mb[rows, :], hid, TN)
-        mg = dot(hid, we128[...], NT)
-        dg = norm_back_lanes(mn[rows, :], ms[rows, :], mg) * mask
-        dgu[rows4] = dg.reshape(4, 64, 128)
-        return carry
-
-    lax.fori_loop(0, 8, back_body, 0)
-
-    h_src = (
-        dgu.at[0:3], dgu.at[29:32], dgu.at[:, 0:8, :], dgu.at[:, 56:64, :],
-        dgu.at[0:3, 0:8, :], dgu.at[0:3, 56:64, :], dgu.at[29:32, 0:8, :], dgu.at[29:32, 56:64, :],
-    )
-    h_dst = (
-        hrow.at[1], hrow.at[0], hcol.at[1], hcol.at[0], hcor.at[3], hcor.at[2], hcor.at[1], hcor.at[0],
-    )
-    halo = [remote(h_src[n], h_dst[n], h_s.at[n], h_r.at[n], near(n)) for n in range(8)]
-    for n in range(8):
-        halo[n].start()
-
-    for b in range(3):
-        lanes = slice(b * 128, (b + 1) * 128)
-        g1[b] = acc_e[0:C0, lanes].astype(BF)
-        g1[3 + b] = acc_r[0:C0, lanes].astype(BF)
-    g1[14] = jnp.zeros((96, 128), BF)
-    g1[15] = jnp.zeros((96, 128), BF)
 
     def make_sum(g, r1, p2, r2, p3, ga, s1, t1, s2, t2, s3, t3):
         first = [
@@ -415,9 +372,60 @@
     start2, turn2, spread2, finish2, drain2 = make_sum(
         g2, g2r1, g2p2, g2r2, g2p3, g2a, q1_s, q1_r, q2_s, q2_r, q3_s, q3_r
     )
+    stem_rows = [remote(g3a, g3r.at[row], r1_s.at[k], r1_r.at[k], row_peer(k)) for k in range(1, ROWS)]
+    stem_cols = [remote(g3b, g3c.at[col], r2_s.at[k], r2_r.at[k], col_peer(k)) for k in range(1, COLS)]
+
+    for b in range(4):
+        lanes = slice(b * 128, (b + 1) * 128)
+        part = dot(eg, gp[:, lanes]).astype(BF)
+        for n in range(4):
+            g1[4 * b + n] = part[n * 48 : (n + 1) * 48]
     start1()
 
-    g2[...] = jnp.zeros_like(g2)
+    gb = dot(egt, dwt[...])
+    for i in range(16):
+        for b in range(4):
+            gs[2 * i + b // 2, pl.ds(b % 2, 32, stride=2), :] = gb[i * 32 : (i + 1) * 32, b * 128 : (b + 1) * 128]
+
+    acc_e[...] = jnp.zeros_like(acc_e)
+    acc_r[...] = jnp.zeros_like(acc_r)
+
+    def back_body(b, carry):
+        rows4 = pl.ds(b * 4, 4)
+        rows = pl.ds(pl.multiple_of(b * 256, 256), 256)
+        grad = gs[rows4].reshape(256, 128)
+        grad = norm_back_lanes(dn[rows4].reshape(256, 128), ds[rows, :], grad) * mask
+        gs[rows4] = grad.reshape(4, 64, 128)
+        og = grad.astype(BF)
+        acc_r[...] += dot(og, act[rows, :], TN)
+        hid = (dot(og, wr128[...]) * slope[rows, :].astype(F32)).astype(BF)
+        acc_e[...] += dot(mb[rows, :], hid, TN)
+        mg = dot(hid, we128[...], NT)
+        dg = norm_back_lanes(mn[rows, :], ms[rows, :], mg) * mask
+        dgu[rows4] = dg.reshape(4, 64, 128)
+        return carry
+
+    lax.fori_loop(0, 8, back_body, 0, unroll=4)
+
+    h_src = (
+        dgu.at[0:3], dgu.at[29:32], dgu.at[:, 0:8, :], dgu.at[:, 56:64, :],
+        dgu.at[0:3, 0:8, :], dgu.at[0:3, 56:64, :], dgu.at[29:32, 0:8, :], dgu.at[29:32, 56:64, :],
+    )
+    h_dst = (
+        hrow.at[1], hrow.at[0], hcol.at[1], hcol.at[0], hcor.at[3], hcor.at[2], hcor.at[1], hcor.at[0],
+    )
+    halo = [remote(h_src[n], h_dst[n], h_s.at[n], h_r.at[n], near(n)) for n in range(8)]
+    for n in range(8):
+        halo[n].start()
+
+    turn1()
+    for b in range(3):
+        lanes = slice(b * 128, (b + 1) * 128)
+        for n in range(2):
+            g2[2 * b + n] = acc_e[n * 48 : (n + 1) * 48, lanes].astype(BF)
+            g2[6 + 2 * b + n] = acc_r[n * 48 : (n + 1) * 48, lanes].astype(BF)
+
+    kt[...] = jnp.zeros_like(kt)
     for v in range(7):
 
         def taps_body(jb, acc, v=v):
@@ -435,10 +443,13 @@
 
         sums = lax.fori_loop(0, 8, taps_body, tuple(jnp.zeros((8, 128), F32) for _ in range(7)))
         for u in range(7):
-            at = 48 + 7 * u + v
-            g2[at // 8, at % 8 : at % 8 + 1, :] = jnp.sum(sums[u], axis=0, keepdims=True)
-
-    turn1()
+            kt[7 * u + v : 7 * u + v + 1, :] = jnp.sum(sums[u], axis=0, keepdims=True)
+    g2[12] = kt[0:48].astype(BF)
+    g2[13] = kt[48:96].astype(BF)
+    g2[14] = jnp.zeros((48, 128), BF)
+    g2[15] = jnp.zeros((48, 128), BF)
+    start2()
+    spread1()
 
     dgp[...] = jnp.zeros_like(dgp)
     for i in range(32):
@@ -458,7 +469,7 @@
     dgp[4:36, 67:70, :] = hcol[1, :, 0:3, :] * right
 
     depthwise(dgp, kb, conv, True)
-    spread1()
+    turn2()
 
     acc_s[...] = jnp.zeros_like(acc_s)
 
@@ -474,7 +485,7 @@
             acc_s[s * 48 : (s + 1) * 48, :] += dot(ft[g, s * 48 : (s + 1) * 48, :], grads)
         return carry
 
-    lax.fori_loop(0, 8, stem_back, 0)
+    lax.fori_loop(0, 8, stem_back, 0, unroll=4)
     rows = iota((192, 128), 0)
     folded = jnp.zeros((192, 128), F32)
     for i4 in range(4):
@@ -483,34 +494,57 @@
     rem = q192 % 48
     gather = (m48 == (rem // 16) * 16 + (rem % 4) * 4 + q192 // 48).astype(F32)
     stem = lax.dot_general(gather, folded, NN, precision=lax.Precision.HIGHEST, preferred_element_type=F32)
-    for n in range(6):
-        g2[n] = stem[n * 8 : (n + 1) * 8]
-
-    start2()
+    g3a[...] = stem.astype(BF)
+    g3r[row] = stem.astype(BF)
+    for cp in stem_rows:
+        cp.start()
     finish1()
+    for b in range(4):
+        for n in range(4):
+            out_down[n * 48 : (n + 1) * 48, b * C0 : (b + 1) * C0] = g1a[4 * b + n, :, 0:C0].astype(F32)
+    spread2()
+    for cp in stem_rows:
+        cp.wait_recv()
+    total = g3r[0].astype(F32)
+    for k in range(1, ROWS):
+        total = total + g3r[k].astype(F32)
+    g3b[...] = total.astype(BF)
+    g3c[col] = total.astype(BF)
+    for cp in stem_cols:
+        cp.start()
+
+    for b in range(6):
+        lanes = slice(b * 128, (b + 1) * 128)
+        part = dot(nball[0], pgall[0, lanes, :], NT)
+        for j in range(1, COLS // 2):
+            part = part + dot(nball[j], pgall[j, lanes, :], NT)
+        out_owner[0, 0, :, lanes] = part
+
+    finish2()
     for b in range(3):
         lanes = slice(b * 128, (b + 1) * 128)
-        out_expand[:, lanes] = g1a[b].astype(F32)
-        out_reduce[lanes, :] = g1a[3 + b].astype(F32).T
-    for b in range(4):
-        out_down[b * C0 : (b + 1) * C0, 0:96] = g1a[6 + 2 * b].astype(F32).T[0:C0, :]
-        out_down[b * C0 : (b + 1) * C0, 96:192] = g1a[7 + 2 * b].astype(F32).T[0:C0, :]
-    turn2()
-    spread2()
-    finish2()
-    for n in range(6):
-        out_stem[n * 8 : (n + 1) * 8, :] = g2a[n, :, 0:C0]
-    for n in range(6, 16):
-        dkp[(n - 6) * 8 : (n - 5) * 8, :] = g2a[n]
-    out_taps[...] = dkp[...].T[0:C0, 0:49]
+        for n in range(2):
+            at = slice(n * 48, (n + 1) * 48)
+            out_expand[at, lanes] = g2a[2 * b + n].astype(F32)
+            out_reduce[at, lanes] = g2a[6 + 2 * b + n].astype(F32)
+    out_taps[0:48, :] = g2a[12].astype(F32)[:, 0:C0]
+    out_taps[48:49, :] = g2a[13].astype(F32)[0:1, 0:C0]
+    for cp in stem_cols:
+        cp.wait_recv()
+    total = g3c[0].astype(F32)
+    for k in range(1, COLS):
+        total = total + g3c[k].astype(F32)
+    out_stem[...] = total[:, 0:C0]
 
     for n in range(8):
         px[n].wait_send()
         halo[n].wait_send()
     for k in range(1, COLS):
-        back_copy(k).wait_send()
+        back_copy(k // 2, k % 2).wait_send()
     drain1()
     drain2()
+    for cp in stem_rows + stem_cols:
+        cp.wait_send()
 
 
 def on_device(pixels, ws, dk, we, wr, wd, wo, tissue, owners, cot):
@@ -518,36 +552,38 @@
     smem = pl.BlockSpec(memory_space=pltpu.SMEM)
     dma = pltpu.SemaphoreType.DMA
     V = pltpu.VMEM
-    outs = ((48, C0), (C0, 49), (C0, HID), (HID, C0), (4 * C0, C1), (1, 1, C1, E))
-    return pl.pallas_call(
+    outs = ((48, C0), (49, C0), (C0, HID), (C0, HID), (C1, 4 * C0), (1, 1, C1, E))
+    stem, taps, expand, reduce, down, owner = pl.pallas_call(
         kernel,
         out_shape=tuple(jax.ShapeDtypeStruct(s, F32) for s in outs),
         in_specs=[vmem] * 7 + [smem, smem, vmem],
         out_specs=(vmem,) * 6,
         scratch_shapes=[
             V((3, 160, 512), BF), V((288, 512), BF), V((4, 256, 64), BF), V((4, 48, 512), BF), V((48, 128), BF),
-            V((128, 128), F32), V((49, 8, 128), F32), V((128, HID), BF), V((HID, 128), BF),
-            V((512, C1), BF), V((C1, 512), BF),
+            V((49, 8, 128), F32), V((128, HID), BF), V((128, HID), BF), V((C1, 512), BF),
             V((40, 72, 128), F32), V((40, 72, 128), F32), V((40, 72, 128), F32), V((8, 192, 64), BF),
             V((32, 64, 128), F32), V((2048, 128), F32), V((2048, 128), F32), V((2048, 128), BF),
             V((2048, HID), BF), V((2048, HID), BF), V((32, 64, 128), F32), V((2048, 128), F32),
             V((512, 512), BF), V((512, 2048), BF),
-            V((16, E), F32), V((16, 208, 128), BF), V((16, 208, 128), BF), V((16, C1, 128), BF), V((C1, 2048), BF),
+            V((16, E), F32), V((16, 208, 128), BF), V((8, 208, 256), BF), V((8, C1, 256), BF), V((C1, 2048), BF),
+            V((8, C1, 256), BF), V((8, E, 256), BF),
             V((E, C1), BF), V((32, 64, 128), F32), V((32, 64, 128), F32), V((40, 72, 128), F32),
             V((2, 3, 64, 128), F32), V((2, 32, 8, 128), F32), V((4, 3, 8, 128), F32),
             V((192, 512), F32), V((128, HID), F32), V((128, HID), F32),
-            V((16, 96, 128), BF), V((16, 96, 128), BF), V((96, 128), BF), V((8, 96, 128), BF), V((96, 128), BF),
-            V((16, 96, 128), BF),
-            V((16, 8, 128), F32), V((16, 8, 128), F32), V((8, 128), F32), V((8, 8, 128), F32), V((8, 128), F32),
-            V((16, 8, 128), F32),
+            V((16, 48, 128), BF), V((16, 48, 128), BF), V((48, 128), BF), V((8, 48, 128), BF), V((48, 128), BF),
+            V((16, 48, 128), BF),
+            V((16, 48, 128), BF), V((16, 48, 128), BF), V((48, 128), BF), V((8, 48, 128), BF), V((48, 128), BF),
+            V((16, 48, 128), BF),
+            V((96, 128), F32), V((48, 128), BF), V((8, 48, 128), BF), V((48, 128), BF), V((16, 48, 128), BF),
             dma((8,)), dma((8,)), dma((16,)), dma((16,)), dma((16,)), dma((16,)), dma((8,)), dma((8,)),
             dma((16,)), dma((16,)), dma((8,)), dma((8,)), dma((16,)), dma((16,)),
-            dma((16,)), dma((16,)), dma((8,)), dma((8,)), dma((16,)), dma((16,)),
+            dma((16,)), dma((16,)), dma((8,)), dma((8,)), dma((16,)), dma((16,)), dma((8,)), dma((8,)), dma((16,)), dma((16,)),
         ],
         compiler_params=pltpu.CompilerParams(
             collective_id=0, has_side_effects=True, vmem_limit_bytes=56 * 1024 * 1024
         ),
-    )(pixels, ws, dk, we, wr, wd, wo, tissue, owners, cot)
+    )(pixels, ws, dk.T, we, wr.T, wd.T, wo, tissue, owners.reshape(1, 8), cot)
+    return stem, taps.T, expand, reduce.T, down.T, owner
 
 
 def solution(mesh):

time: 124 us -> 96.6 us (0.78)
  Pallas kernels: 112 us -> 90 us
  local copies, waits for them, and re-layouts: 11.5 us -> 5.84 us
    pallas_call x1, Pallas kernels: 112 us -> 90 us  [on_device(): pl.pallas_call(kernel, out_shape=tuple((jax.ShapeDtypeStruct(s, F32) for...]
    pallas_call x3 -> x0, local copies, waits for them, and re-layouts: 4.13 us -> none  [on_device(): pl.pallas_call(kernel, out_shape=tuple((jax.ShapeDtypeStruct(s, F32) for...]
    unnamed x17 -> x14, local copies, waits for them, and re-layouts: 7.37 us -> 5.84 us
where the time goes in v2:
time: 96.6 us; the launch traced here: 96.5 us
  Pallas kernels  90 us (93%)
  local copies, waits for them, and re-layouts  5.84 us (6%)
    pallas_call x1, Pallas kernels, on_device(): pl.pallas_call(kernel, out_shape=tuple((jax.ShapeDtypeStruct(s, F32) for...  90 us
    unnamed x14, local copies, waits for them, and re-layouts  5.84 us

profile of v2, /device:TPU:1, one launch (start us, length us, event | category | flops | bytes accessed | tf_op | source)
XLA Modules:
  0.0 96.5 jit_solution(6680603439153087091)
XLA Ops:
  0.6 90.0 %shard_map.145 = (f32[48,96]{1,0:T(8,128)}, f32[49,96]{1,0:T(8,128)}, f32[96,384]{1,0:T(8,128)}, f32[96,384]{1,0:T(8,128)}, f32[192,384]{1,0:T(8,128)}, /*index=5*/f32[1,1,192,768]{3,2,1,0:T(8,128)}) custom-call(bf16[3,128,256]{2,1,0:T(8,128)(2,1)} %pix.1, bf16[48,96]{1,0:T(8,128)(2,1)} %ws.1, f32[49,96]{1,0:T(8,128)} %bitcast.12, bf16[96,384]{1,0:T(8,128)(2,1)} %we.1, ...), custom_call_target="tpu_custom_call" | custom-call | tf_op jit(solution)/shard_map/pallas_call | solution.py:556
  90.6 0.0 copy-start.3
  90.6 0.0 copy-start.2
  90.6 1.4 %copy.22 = f32[48,96]{1,0:T(8,128)} copy(f32[48,96]{1,0:T(8,128)} %get-tuple-element.24) | data formatting | bytes 36864
  92.0 0.0 copy-done.3
  92.0 0.0 copy-start.1
  92.0 0.6 copy.23
  92.6 0.0 copy-start
  92.6 1.6 %copy.24 = f32[96,384]{1,0:T(8,128)} copy(f32[96,384]{1,0:T(8,128)} %get-tuple-element.26) | data formatting | bytes 294912
  94.3 0.0 copy-done.2
  94.3 0.7 copy.25
  94.9 0.0 copy-done.1
  94.9 0.7 copy.26
  95.6 0.0 copy-done
  95.6 0.8 copy.27
Async XLA Ops:
  90.6 1.4 %copy-start.3 = (f32[49,96]{1,0:T(8,128)S(1)}, f32[49,96]{1,0:T(8,128)}, u32[]{:S(2)}) copy-start(f32[49,96]{1,0:T(8,128)} %get-tuple-element.13) | copy-start | bytes 56452
  90.6 3.7 %copy-start.2 = (f32[96,384]{1,0:T(8,128)S(1)}, f32[96,384]{1,0:T(8,128)}, u32[]{:S(2)}) copy-start(f32[96,384]{1,0:T(8,128)} %get-tuple-element.15) | copy-start | bytes 442372
  92.0 2.9 %copy-start.1 = (f32[192,384]{1,0:T(8,128)S(1)}, f32[192,384]{1,0:T(8,128)}, u32[]{:S(2)}) copy-start(f32[192,384]{1,0:T(8,128)} %get-tuple-element.16) | copy-start | bytes 884740
  92.6 3.0 %copy-start = (f32[1,1,192,768]{3,2,1,0:T(8,128)S(1)}, f32[1,1,192,768]{3,2,1,0:T(8,128)}, u32[]{:S(2)}) copy-start(f32[1,1,192,768]{3,2,1,0:T(8,128)} %get-tuple-element.29) | copy-start | bytes 1769476

commit v3 on v2

--- a/solution.py
+++ b/solution.py
@@ -47,9 +47,9 @@
     return h * half, half + 0.5 * h * (1.0 - t * t) * (SLOPE * (1.0 + 3.0 * CUBIC * sq))
 
 
-def depthwise(src, kb, dst, flip):
+def depthwise(src, kb, dst, flip, count=32, tile=lambda n: (n // 8, n % 8)):
     def body(n, carry):
-        ib, jb = n // 8, n % 8
+        ib, jb = tile(n)
         i0 = ib * 8
         acc = [None] * 8
         for v in range(7):
@@ -68,19 +68,20 @@
             dst[i0 + i, pl.ds(pl.multiple_of(jb * 8, 8), 8), :] = acc[i]
         return carry
 
-    lax.fori_loop(0, 32, body, 0)
+    lax.fori_loop(0, count, body, 0, unroll=2)
 
 
 def kernel(
     pix, ws, dkt, we, wrt, wdt, wo, tissue, owners, cot,
     out_stem, out_taps, out_expand, out_reduce, out_down, out_owner,
-    xe, perm, permi, wblk, ws128, kb, we128, wr128, dwt,
+    xe, perm, perms, permi, wblk, ws128, kb, we128, wr128, dwt,
     pad, sn, ss, ft, conv, mn, ms, mb, act, slope, dn, ds, gp, pmt,
     cots, sbuf, rbuf, rets, ret, nball, pgall, wt, gs, dgu, dgp, hrow, hcol, hcor,
     acc_s, acc_e, acc_r,
-    g1, g1r1, g1p2, g1r2, g1p3, g1a, g2, g2r1, g2p2, g2r2, g2p3, g2a, kt, g3a, g3r, g3b, g3c,
+    g1, g1r1, g1p2, g1r2, g1p3, g1a, g2, g2r1, g2p2, g2r2, g2p3, g2a, kt, g3s, g3t, g3a, g3r, g3b, g3c, g4a, g4r, g4b, g4c,
     px_s, px_r, a_s, a_r, b_s, b_r, h_s, h_r,
     p1_s, p1_r, p2_s, p2_r, p3_s, p3_r, q1_s, q1_r, q2_s, q2_r, q3_s, q3_r, r1_s, r1_r, r2_s, r2_r,
+    r0_s, r0_r, t1_s, t1_r, t2_s, t2_r,
 ):
     row, col = lax.axis_index("row"), lax.axis_index("col")
 
@@ -121,9 +122,12 @@
         px[n].start()
 
     mask = (iota((1, 128), 1) < C0).astype(F32)
-    xe[:, 16:144, 128:384] = pix[...]
-    pr = iota((288, 512), 0)
-    perm[...] = (iota((288, 512), 1) == 116 + 4 * (pr % 72) + pr // 72).astype(F32).astype(BF)
+    pr = iota((256, 256), 0)
+    perm[...] = (iota((256, 256), 1) == 4 * (pr % 64) + pr // 64).astype(F32).astype(BF)
+    pr = iota((32, 128), 0)
+    pl_ = iota((32, 128), 1)
+    perms[0] = jnp.where(pr % 8 < 3, (pl_ == 116 + 4 * (pr % 8) + pr // 8).astype(F32), 0.0).astype(BF)
+    perms[1] = jnp.where(pr % 8 < 3, (pl_ == 4 * (pr % 8) + pr // 8).astype(F32), 0.0).astype(BF)
     for s in range(4):
         permi[s] = (iota((256, 64), 0) == 4 * iota((256, 64), 1) + s).astype(F32).astype(BF)
     ws128[...] = jnp.zeros_like(ws128)
@@ -145,7 +149,27 @@
     dwt[...] = jnp.zeros_like(dwt)
     for b in range(4):
         dwt[:, b * 128 : b * 128 + C0] = wdt[:, b * C0 : (b + 1) * C0]
-    wt[...] = wo[0, 0].astype(F32).T.astype(BF)
+
+    def stem_piece(ref, r0, lanes, chooser, width, use):
+        at = pl.ds(pl.multiple_of(r0, 16), 16)
+        xg = jnp.concatenate([ref[0, at, lanes], ref[1, at, lanes], ref[2, at, lanes]], axis=0)
+        turned = dot(chooser, xg, NT)
+        total = jnp.zeros((width, 512), F32)
+        for s in range(4):
+            total = total + dot(turned[s * width : (s + 1) * width].astype(BF), wblk[s])
+        for i4 in range(4):
+            use(i4, *norm_lanes(total[:, i4 * 128 : (i4 + 1) * 128], mask))
+
+    def stem_body(g, carry):
+        def use(i4, normed, scale):
+            pad[4 * g + 4 + i4, 3:67, :] = normed.astype(BF).astype(F32)
+            sn[4 * g + i4] = normed
+            ss[4 * g + i4] = jnp.broadcast_to(scale, (64, 128))
+
+        stem_piece(pix, g * 16, slice(0, 256), perm[...], 64, use)
+        return carry
+
+    lax.fori_loop(0, 8, stem_body, 0, unroll=8)
 
     slots = []
     for p in range(8):
@@ -200,30 +224,21 @@
     def _():
         xe[:, :, 384:512] = jnp.zeros((3, 160, 128), BF)
 
-    def stem_body(g, carry):
-        at = pl.ds(pl.multiple_of(g * 16, 16), 16)
-        xg = jnp.concatenate([xe[0, at, :], xe[1, at, :], xe[2, at, :]], axis=0)
-        turned = dot(perm[...], xg, NT)
-        total = jnp.zeros((72, 512), F32)
-        for s in range(4):
-            total = total + dot(turned[s * 72 : (s + 1) * 72].astype(BF), wblk[s])
-        for i4 in range(4):
-            normed, scale = norm_lanes(total[:, i4 * 128 : (i4 + 1) * 128], mask)
-            pad[4 * g + i4] = normed.astype(BF).astype(F32)
-            sn[4 * g + i4] = normed
-            ss[4 * g + i4] = jnp.broadcast_to(scale, (72, 128))
-        return carry
-
-    lax.fori_loop(0, 10, stem_body, 0, unroll=10)
-
-    def flat_body(g, carry):
-        at = pl.ds(pl.multiple_of(g * 16 + 16, 16), 16)
-        xg = jnp.concatenate([xe[0, at, 128:384], xe[1, at, 128:384], xe[2, at, 128:384]], axis=0)
-        for s in range(4):
-            ft[g, s * 48 : (s + 1) * 48, :] = dot(xg, permi[s]).astype(BF)
-        return carry
-
-    lax.fori_loop(0, 8, flat_body, 0, unroll=8)
+    def side_body(g, carry):
+        for side in range(2):
+            def use(i4, normed, scale, side=side):
+                pad[4 * g + i4, side * 67 : side * 67 + 3, :] = normed[0:3].astype(BF).astype(F32)
+
+            stem_piece(xe, g * 16, slice(side * 384, side * 384 + 128), perms[side], 8, use)
+        return carry
+
+    lax.fori_loop(0, 10, side_body, 0, unroll=10)
+    for g in (0, 9):
+
+        def use(i4, normed, scale, g=g):
+            pad[4 * g + i4, 3:67, :] = normed.astype(BF).astype(F32)
+
+        stem_piece(xe, g * 16, slice(128, 384), perm[...], 64, use)
 
     depthwise(pad, kb, conv, False)
 
@@ -300,6 +315,16 @@
         proj = jnp.sum(back * normed, axis=0, keepdims=True) * (1.0 / C1)
         rets[j] = (scale * (back - mean - normed * proj)).astype(BF)
 
+    wt[...] = wo[0, 0].astype(F32).T.astype(BF)
+    def flat_body(g, carry):
+        at = pl.ds(pl.multiple_of(g * 16, 16), 16)
+        xg = jnp.concatenate([pix[0, at, :], pix[1, at, :], pix[2, at, :]], axis=0)
+        for s in range(4):
+            ft[g, s * 48 : (s + 1) * 48, :] = dot(xg, permi[s]).astype(BF)
+        return carry
+
+    lax.fori_loop(0, 8, flat_body, 0, unroll=8)
+
     out_copy(1).wait_recv()
     own(0)
     ret[:, mine] = rets[0, :, 0:128]
@@ -372,8 +397,15 @@
     start2, turn2, spread2, finish2, drain2 = make_sum(
         g2, g2r1, g2p2, g2r2, g2p3, g2a, q1_s, q1_r, q2_s, q2_r, q3_s, q3_r
     )
+    tap_rows = [remote(g4a, g4r.at[row], t1_s.at[k], t1_r.at[k], row_peer(k)) for k in range(1, ROWS)]
+    tap_cols = [remote(g4b, g4c.at[col], t2_s.at[k], t2_r.at[k], col_peer(k)) for k in range(1, COLS)]
     stem_rows = [remote(g3a, g3r.at[row], r1_s.at[k], r1_r.at[k], row_peer(k)) for k in range(1, ROWS)]
-    stem_cols = [remote(g3b, g3c.at[col], r2_s.at[k], r2_r.at[k], col_peer(k)) for k in range(1, COLS)]
+    core = lax.rem(col, 2)
+    half = (col - core) // 2
+    stem_pair = remote(g3s, g3t, r0_s.at[0], r0_r.at[0], (row, col + 1 - 2 * core))
+    stem_cols = [
+        remote(g3b, g3c.at[half], r2_s.at[k], r2_r.at[k], (row, lax.rem(col + 2 * k, COLS))) for k in range(1, COLS // 2)
+    ]
 
     for b in range(4):
         lanes = slice(b * 128, (b + 1) * 128)
@@ -405,7 +437,7 @@
         dgu[rows4] = dg.reshape(4, 64, 128)
         return carry
 
-    lax.fori_loop(0, 8, back_body, 0, unroll=4)
+    lax.fori_loop(0, 8, back_body, 0, unroll=8)
 
     h_src = (
         dgu.at[0:3], dgu.at[29:32], dgu.at[:, 0:8, :], dgu.at[:, 56:64, :],
@@ -424,6 +456,9 @@
         for n in range(2):
             g2[2 * b + n] = acc_e[n * 48 : (n + 1) * 48, lanes].astype(BF)
             g2[6 + 2 * b + n] = acc_r[n * 48 : (n + 1) * 48, lanes].astype(BF)
+    for n in range(12, 16):
+        g2[n] = jnp.zeros((48, 128), BF)
+    start2()
 
     kt[...] = jnp.zeros_like(kt)
     for v in range(7):
@@ -444,16 +479,15 @@
         sums = lax.fori_loop(0, 8, taps_body, tuple(jnp.zeros((8, 128), F32) for _ in range(7)))
         for u in range(7):
             kt[7 * u + v : 7 * u + v + 1, :] = jnp.sum(sums[u], axis=0, keepdims=True)
-    g2[12] = kt[0:48].astype(BF)
-    g2[13] = kt[48:96].astype(BF)
-    g2[14] = jnp.zeros((48, 128), BF)
-    g2[15] = jnp.zeros((48, 128), BF)
-    start2()
+    g4a[...] = kt[...].astype(BF)
+    g4r[row] = kt[...].astype(BF)
+    for cp in tap_rows:
+        cp.start()
     spread1()
 
-    dgp[...] = jnp.zeros_like(dgp)
     for i in range(32):
         dgp[4 + i, 3:67, :] = dgu[i]
+    depthwise(dgp, kb, conv, True, 12, lambda n: (1 + n // 6, 1 + n % 6))
     for n in range(8):
         halo[n].wait_recv()
     top, bottom = jnp.where(row > 0, 1.0, 0.0), jnp.where(row < ROWS - 1, 1.0, 0.0)
@@ -468,8 +502,19 @@
     dgp[4:36, 0:3, :] = hcol[0, :, 5:8, :] * left
     dgp[4:36, 67:70, :] = hcol[1, :, 0:3, :] * right
 
-    depthwise(dgp, kb, conv, True)
     turn2()
+    depthwise(dgp, kb, conv, True, 16, lambda n: ((n // 8) * 3, n % 8))
+    depthwise(dgp, kb, conv, True, 4, lambda n: (1 + n // 2, (n % 2) * 7))
+    for cp in tap_rows:
+        cp.wait_recv()
+    total = g4r[0].astype(F32)
+    for k in range(1, ROWS):
+        total = total + g4r[k].astype(F32)
+    g4b[...] = total.astype(BF)
+    g4c[col] = total.astype(BF)
+    for cp in tap_cols:
+        cp.start()
+    spread2()
 
     acc_s[...] = jnp.zeros_like(acc_s)
 
@@ -478,7 +523,7 @@
         for i in range(4):
             grad = gs[4 * g + i] + conv[4 * g + i]
             parts.append(
-                norm_back_lanes(sn[4 * g + 4 + i, 3:67, :], ss[4 * g + 4 + i, 3:67, :], grad).astype(BF)
+                norm_back_lanes(sn[4 * g + i], ss[4 * g + i], grad).astype(BF)
             )
         grads = jnp.concatenate(parts, axis=1)
         for s in range(4):
@@ -494,22 +539,25 @@
     rem = q192 % 48
     gather = (m48 == (rem // 16) * 16 + (rem % 4) * 4 + q192 // 48).astype(F32)
     stem = lax.dot_general(gather, folded, NN, precision=lax.Precision.HIGHEST, preferred_element_type=F32)
-    g3a[...] = stem.astype(BF)
-    g3r[row] = stem.astype(BF)
+    g3s[...] = stem.astype(BF)
+    stem_pair.start()
+    stem_pair.wait_recv()
+    stem = (g3s[...].astype(F32) + g3t[...].astype(F32)).astype(BF)
+    g3a[...] = stem
+    g3r[row] = stem
     for cp in stem_rows:
         cp.start()
     finish1()
     for b in range(4):
         for n in range(4):
             out_down[n * 48 : (n + 1) * 48, b * C0 : (b + 1) * C0] = g1a[4 * b + n, :, 0:C0].astype(F32)
-    spread2()
     for cp in stem_rows:
         cp.wait_recv()
     total = g3r[0].astype(F32)
     for k in range(1, ROWS):
         total = total + g3r[k].astype(F32)
     g3b[...] = total.astype(BF)
-    g3c[col] = total.astype(BF)
+    g3c[half] = total.astype(BF)
     for cp in stem_cols:
         cp.start()
 
@@ -527,12 +575,16 @@
             at = slice(n * 48, (n + 1) * 48)
             out_expand[at, lanes] = g2a[2 * b + n].astype(F32)
             out_reduce[at, lanes] = g2a[6 + 2 * b + n].astype(F32)
-    out_taps[0:48, :] = g2a[12].astype(F32)[:, 0:C0]
-    out_taps[48:49, :] = g2a[13].astype(F32)[0:1, 0:C0]
+    for cp in tap_cols:
+        cp.wait_recv()
+    total = g4c[0].astype(F32)
+    for k in range(1, COLS):
+        total = total + g4c[k].astype(F32)
+    out_taps[...] = total[0:49, 0:C0]
     for cp in stem_cols:
         cp.wait_recv()
     total = g3c[0].astype(F32)
-    for k in range(1, COLS):
+    for k in range(1, COLS // 2):
         total = total + g3c[k].astype(F32)
     out_stem[...] = total[:, 0:C0]
 
@@ -543,8 +595,13 @@
         back_copy(k // 2, k % 2).wait_send()
     drain1()
     drain2()
-    for cp in stem_rows + stem_cols:
+    for cp in [stem_pair] + stem_rows + stem_cols + tap_rows + tap_cols:
         cp.wait_send()
+
+
+def hand_over(*refs):
+    for n in range(6):
+        refs[6 + n][...] = refs[n][...].astype(F32)
 
 
 def on_device(pixels, ws, dk, we, wr, wd, wo, tissue, owners, cot):
@@ -553,15 +610,15 @@
     dma = pltpu.SemaphoreType.DMA
     V = pltpu.VMEM
     outs = ((48, C0), (49, C0), (C0, HID), (C0, HID), (C1, 4 * C0), (1, 1, C1, E))
-    stem, taps, expand, reduce, down, owner = pl.pallas_call(
+    results = pl.pallas_call(
         kernel,
         out_shape=tuple(jax.ShapeDtypeStruct(s, F32) for s in outs),
         in_specs=[vmem] * 7 + [smem, smem, vmem],
         out_specs=(vmem,) * 6,
         scratch_shapes=[
-            V((3, 160, 512), BF), V((288, 512), BF), V((4, 256, 64), BF), V((4, 48, 512), BF), V((48, 128), BF),
+            V((3, 160, 512), BF), V((256, 256), BF), V((2, 32, 128), BF), V((4, 256, 64), BF), V((4, 48, 512), BF), V((48, 128), BF),
             V((49, 8, 128), F32), V((128, HID), BF), V((128, HID), BF), V((C1, 512), BF),
-            V((40, 72, 128), F32), V((40, 72, 128), F32), V((40, 72, 128), F32), V((8, 192, 64), BF),
+            V((40, 72, 128), F32), V((32, 64, 128), F32), V((32, 64, 128), F32), V((8, 192, 64), BF),
             V((32, 64, 128), F32), V((2048, 128), F32), V((2048, 128), F32), V((2048, 128), BF),
             V((2048, HID), BF), V((2048, HID), BF), V((32, 64, 128), F32), V((2048, 128), F32),
             V((512, 512), BF), V((512, 2048), BF),
@@ -574,15 +631,24 @@
             V((16, 48, 128), BF),
             V((16, 48, 128), BF), V((16, 48, 128), BF), V((48, 128), BF), V((8, 48, 128), BF), V((48, 128), BF),
             V((16, 48, 128), BF),
-            V((96, 128), F32), V((48, 128), BF), V((8, 48, 128), BF), V((48, 128), BF), V((16, 48, 128), BF),
+            V((64, 128), F32), V((48, 128), BF), V((48, 128), BF), V((48, 128), BF), V((8, 48, 128), BF), V((48, 128), BF),
+            V((8, 48, 128), BF),
+            V((64, 128), BF), V((8, 64, 128), BF), V((64, 128), BF), V((16, 64, 128), BF),
             dma((8,)), dma((8,)), dma((16,)), dma((16,)), dma((16,)), dma((16,)), dma((8,)), dma((8,)),
             dma((16,)), dma((16,)), dma((8,)), dma((8,)), dma((16,)), dma((16,)),
             dma((16,)), dma((16,)), dma((8,)), dma((8,)), dma((16,)), dma((16,)), dma((8,)), dma((8,)), dma((16,)), dma((16,)),
+            dma((1,)), dma((1,)), dma((8,)), dma((8,)), dma((16,)), dma((16,)),
         ],
         compiler_params=pltpu.CompilerParams(
             collective_id=0, has_side_effects=True, vmem_limit_bytes=56 * 1024 * 1024
         ),
     )(pixels, ws, dk.T, we, wr.T, wd.T, wo, tissue, owners.reshape(1, 8), cot)
+    stem, taps, expand, reduce, down, owner = pl.pallas_call(
+        hand_over,
+        out_shape=tuple(jax.ShapeDtypeStruct(s, F32) for s in outs),
+        in_specs=[vmem] * 6,
+        out_specs=(vmem,) * 6,
+    )(*results)
     return stem, taps.T, expand, reduce.T, down.T, owner
 
 

time: 96.6 us -> 94.8 us (0.981)
  local copies, waits for them, and re-layouts: 5.84 us -> 0 us
  Pallas kernels: 90 us -> 94 us
    unnamed x14 -> x0, local copies, waits for them, and re-layouts: 5.84 us -> none
    pallas_call x0 -> x1, Pallas kernels: none -> 2.38 us  [on_device(): pl.pallas_call(hand_over, out_shape=tuple((jax.ShapeDtypeStruct(s, F32) f...]
    pallas_call x1, Pallas kernels: 90 us -> 91.6 us  [on_device(): pl.pallas_call(kernel, out_shape=tuple((jax.ShapeDtypeStruct(s, F32) for...]
where the time goes in v3:
time: 94.8 us; the launch traced here: 94.6 us
  Pallas kernels  94 us (99%)
    pallas_call x1, Pallas kernels, on_device(): pl.pallas_call(kernel, out_shape=tuple((jax.ShapeDtypeStruct(s, F32) for...  91.6 us
    pallas_call x1, Pallas kernels, on_device(): pl.pallas_call(hand_over, out_shape=tuple((jax.ShapeDtypeStruct(s, F32) f...  2.38 us

profile of v3, /device:TPU:1, one launch (start us, length us, event | category | flops | bytes accessed | tf_op | source)
XLA Modules:
  0.0 94.6 jit_solution(8088516260910528371)
XLA Ops:
  0.6 91.6 %shard_map.145 = (f32[48,96]{1,0:T(8,128)}, f32[49,96]{1,0:T(8,128)}, f32[96,384]{1,0:T(8,128)}, f32[96,384]{1,0:T(8,128)}, f32[192,384]{1,0:T(8,128)}, /*index=5*/f32[1,1,192,768]{3,2,1,0:T(8,128)}) custom-call(bf16[3,128,256]{2,1,0:T(8,128)(2,1)} %pix.1, bf16[48,96]{1,0:T(8,128)(2,1)} %ws.1, f32[49,96]{1,0:T(8,128)} %bitcast.9, bf16[96,384]{1,0:T(8,128)(2,1)} %we.1, ...), custom_call_target="tpu_custom_call" | custom-call | tf_op jit(solution)/shard_map/pallas_call | solution.py:613
  92.2 2.4 %shard_map.146 = (f32[48,96]{1,0:T(8,128)}, f32[49,96]{1,0:T(8,128)}, f32[96,384]{1,0:T(8,128)}, f32[96,384]{1,0:T(8,128)}, f32[192,384]{1,0:T(8,128)}, /*index=5*/f32[1,1,192,768]{3,2,1,0:T(8,128)}) custom-call(f32[48,96]{1,0:T(8,128)} %get-tuple-element.18.refs_0_, f32[49,96]{1,0:T(8,128)} %get-tuple-element.19.refs_1_, ...), custom_call_target="tpu_custom_call" | custom-call | tf_op jit(solution)/shard_map/pallas_call | solution.py:646

commit v4 on v3

--- a/solution.py
+++ b/solution.py
@@ -76,7 +76,7 @@
     out_stem, out_taps, out_expand, out_reduce, out_down, out_owner,
     xe, perm, perms, permi, wblk, ws128, kb, we128, wr128, dwt,
     pad, sn, ss, ft, conv, mn, ms, mb, act, slope, dn, ds, gp, pmt,
-    cots, sbuf, rbuf, rets, ret, nball, pgall, wt, gs, dgu, dgp, hrow, hcol, hcor,
+    cots, sbuf, rbuf, rets, ret, nball, pgall, wt, gs, dgu, dgp, hsr, hsc, hrow, hcol, hcor,
     acc_s, acc_e, acc_r,
     g1, g1r1, g1p2, g1r2, g1p3, g1a, g2, g2r1, g2p2, g2r2, g2p3, g2a, kt, g3s, g3t, g3a, g3r, g3b, g3c, g4a, g4r, g4b, g4c,
     px_s, px_r, a_s, a_r, b_s, b_r, h_s, h_r,
@@ -439,8 +439,13 @@
 
     lax.fori_loop(0, 8, back_body, 0, unroll=8)
 
+    hsr[0] = dgu[0:3].reshape(192, 128).astype(BF)
+    hsr[1] = dgu[29:32].reshape(192, 128).astype(BF)
+    for n in range(3):
+        hsc[0, n * 32 : (n + 1) * 32, :] = dgu[:, n, :].astype(BF)
+        hsc[1, n * 32 : (n + 1) * 32, :] = dgu[:, 61 + n, :].astype(BF)
     h_src = (
-        dgu.at[0:3], dgu.at[29:32], dgu.at[:, 0:8, :], dgu.at[:, 56:64, :],
+        hsr.at[0], hsr.at[1], hsc.at[0], hsc.at[1],
         dgu.at[0:3, 0:8, :], dgu.at[0:3, 56:64, :], dgu.at[29:32, 0:8, :], dgu.at[29:32, 56:64, :],
     )
     h_dst = (
@@ -493,14 +498,15 @@
     top, bottom = jnp.where(row > 0, 1.0, 0.0), jnp.where(row < ROWS - 1, 1.0, 0.0)
     left, right = jnp.where(col > 0, 1.0, 0.0), jnp.where(col < COLS - 1, 1.0, 0.0)
     for i in range(3):
-        dgp[1 + i, 3:67, :] = hrow[0, i] * top
-        dgp[36 + i, 3:67, :] = hrow[1, i] * bottom
+        dgp[1 + i, 3:67, :] = hrow[0, i * 64 : (i + 1) * 64, :].astype(F32) * top
+        dgp[36 + i, 3:67, :] = hrow[1, i * 64 : (i + 1) * 64, :].astype(F32) * bottom
         dgp[1 + i, 0:3, :] = hcor[0, i, 5:8] * (top * left)
         dgp[1 + i, 67:70, :] = hcor[1, i, 0:3] * (top * right)
         dgp[36 + i, 0:3, :] = hcor[2, i, 5:8] * (bottom * left)
         dgp[36 + i, 67:70, :] = hcor[3, i, 0:3] * (bottom * right)
-    dgp[4:36, 0:3, :] = hcol[0, :, 5:8, :] * left
-    dgp[4:36, 67:70, :] = hcol[1, :, 0:3, :] * right
+    for n in range(3):
+        dgp[4:36, n, :] = hcol[0, n * 32 : (n + 1) * 32, :].astype(F32) * left
+        dgp[4:36, 67 + n, :] = hcol[1, n * 32 : (n + 1) * 32, :].astype(F32) * right
 
     turn2()
     depthwise(dgp, kb, conv, True, 16, lambda n: ((n // 8) * 3, n % 8))
@@ -625,7 +631,7 @@
             V((16, E), F32), V((16, 208, 128), BF), V((8, 208, 256), BF), V((8, C1, 256), BF), V((C1, 2048), BF),
             V((8, C1, 256), BF), V((8, E, 256), BF),
             V((E, C1), BF), V((32, 64, 128), F32), V((32, 64, 128), F32), V((40, 72, 128), F32),
-            V((2, 3, 64, 128), F32), V((2, 32, 8, 128), F32), V((4, 3, 8, 128), F32),
+            V((2, 192, 128), BF), V((2, 96, 128), BF), V((2, 192, 128), BF), V((2, 96, 128), BF), V((4, 3, 8, 128), F32),
             V((192, 512), F32), V((128, HID), F32), V((128, HID), F32),
             V((16, 48, 128), BF), V((16, 48, 128), BF), V((48, 128), BF), V((8, 48, 128), BF), V((48, 128), BF),
             V((16, 48, 128), BF),

time: 94.8 us -> 92.1 us (0.972)
  Pallas kernels: 94 us -> 90.9 us
    pallas_call x1, Pallas kernels: 91.6 us -> 88.5 us  [on_device(): pl.pallas_call(kernel, out_shape=tuple((jax.ShapeDtypeStruct(s, F32) for...]
where the time goes in v4:
time: 92.1 us; the launch traced here: 91.5 us
  Pallas kernels  90.9 us (99%)
    pallas_call x1, Pallas kernels, on_device(): pl.pallas_call(kernel, out_shape=tuple((jax.ShapeDtypeStruct(s, F32) for...  88.5 us
    pallas_call x1, Pallas kernels, on_device(): pl.pallas_call(hand_over, out_shape=tuple((jax.ShapeDtypeStruct(s, F32) f...  2.38 us

profile of v4, /device:TPU:1, one launch (start us, length us, event | category | flops | bytes accessed | tf_op | source)
XLA Modules:
  0.0 91.5 jit_solution(12540481884952393486)
XLA Ops:
  0.6 88.5 %shard_map.145 = (f32[48,96]{1,0:T(8,128)}, f32[49,96]{1,0:T(8,128)}, f32[96,384]{1,0:T(8,128)}, f32[96,384]{1,0:T(8,128)}, f32[192,384]{1,0:T(8,128)}, /*index=5*/f32[1,1,192,768]{3,2,1,0:T(8,128)}) custom-call(bf16[3,128,256]{2,1,0:T(8,128)(2,1)} %pix.1, bf16[48,96]{1,0:T(8,128)(2,1)} %ws.1, f32[49,96]{1,0:T(8,128)} %bitcast.9, bf16[96,384]{1,0:T(8,128)(2,1)} %we.1, ...), custom_call_target="tpu_custom_call" | custom-call | tf_op jit(solution)/shard_map/pallas_call | solution.py:619
  89.1 2.4 %shard_map.146 = (f32[48,96]{1,0:T(8,128)}, f32[49,96]{1,0:T(8,128)}, f32[96,384]{1,0:T(8,128)}, f32[96,384]{1,0:T(8,128)}, f32[192,384]{1,0:T(8,128)}, /*index=5*/f32[1,1,192,768]{3,2,1,0:T(8,128)}) custom-call(f32[48,96]{1,0:T(8,128)} %get-tuple-element.18.refs_0_, f32[49,96]{1,0:T(8,128)} %get-tuple-element.19.refs_1_, ...), custom_call_target="tpu_custom_call" | custom-call | tf_op jit(solution)/shard_map/pallas_call | solution.py:652

commit v5 on v4

--- a/solution.py
+++ b/solution.py
@@ -110,15 +110,17 @@
     pl.semaphore_wait(barrier, (COLS - 1) + (ROWS - 1) + 4)
 
     px_src = (
-        pix.at[:, 0:16, :], pix.at[:, 112:128, :], pix.at[:, :, 0:128], pix.at[:, :, 128:256],
+        pix.at[:, 0:16, :], pix.at[:, 112:128, :], pix.at[:, 0:64, 0:128], pix.at[:, 0:64, 128:256],
         pix.at[:, 0:16, 0:128], pix.at[:, 0:16, 128:256], pix.at[:, 112:128, 0:128], pix.at[:, 112:128, 128:256],
+        pix.at[:, 64:128, 0:128], pix.at[:, 64:128, 128:256],
     )
     px_dst = (
-        xe.at[:, 144:160, 128:384], xe.at[:, 0:16, 128:384], xe.at[:, 16:144, 384:512], xe.at[:, 16:144, 0:128],
+        xe.at[:, 144:160, 128:384], xe.at[:, 0:16, 128:384], xe.at[:, 16:80, 384:512], xe.at[:, 16:80, 0:128],
         xe.at[:, 144:160, 384:512], xe.at[:, 144:160, 0:128], xe.at[:, 0:16, 384:512], xe.at[:, 0:16, 0:128],
-    )
-    px = [remote(px_src[n], px_dst[n], px_s.at[n], px_r.at[n], near(n)) for n in range(8)]
-    for n in range(8):
+        xe.at[:, 80:144, 384:512], xe.at[:, 80:144, 0:128],
+    )
+    px = [remote(px_src[n], px_dst[n], px_s.at[n], px_r.at[n], near(n if n < 8 else n - 6)) for n in range(10)]
+    for n in (2, 3, 8, 9, 0, 1, 4, 5, 6, 7):
         px[n].start()
 
     mask = (iota((1, 128), 1) < C0).astype(F32)
@@ -205,7 +207,7 @@
     for d in range(COLS):
         sbuf[d, C1 : C1 + 16, :] = packed[d * 16 : (d + 1) * 16].astype(BF)
 
-    for n in range(8):
+    for n in range(10):
         px[n].wait_recv()
 
     @pl.when(row == 0)
@@ -594,8 +596,9 @@
         total = total + g3c[k].astype(F32)
     out_stem[...] = total[:, 0:C0]
 
+    for n in range(10):
+        px[n].wait_send()
     for n in range(8):
-        px[n].wait_send()
         halo[n].wait_send()
     for k in range(1, COLS):
         back_copy(k // 2, k % 2).wait_send()
@@ -640,7 +643,7 @@
             V((64, 128), F32), V((48, 128), BF), V((48, 128), BF), V((48, 128), BF), V((8, 48, 128), BF), V((48, 128), BF),
             V((8, 48, 128), BF),
             V((64, 128), BF), V((8, 64, 128), BF), V((64, 128), BF), V((16, 64, 128), BF),
-            dma((8,)), dma((8,)), dma((16,)), dma((16,)), dma((16,)), dma((16,)), dma((8,)), dma((8,)),
+            dma((10,)), dma((10,)), dma((16,)), dma((16,)), dma((16,)), dma((16,)), dma((8,)), dma((8,)),
             dma((16,)), dma((16,)), dma((8,)), dma((8,)), dma((16,)), dma((16,)),
             dma((16,)), dma((16,)), dma((8,)), dma((8,)), dma((16,)), dma((16,)), dma((8,)), dma((8,)), dma((16,)), dma((16,)),
             dma((1,)), dma((1,)), dma((8,)), dma((8,)), dma((16,)), dma((16,)),

time: 92.1 us -> 91 us (0.988)
  no operation moved by 1% of the time
where the time goes in v5:
time: 91 us; the launch traced here: 90.8 us
  Pallas kernels  90.2 us (99%)
    pallas_call x1, Pallas kernels, on_device(): pl.pallas_call(kernel, out_shape=tuple((jax.ShapeDtypeStruct(s, F32) for...  87.8 us
    pallas_call x1, Pallas kernels, on_device(): pl.pallas_call(hand_over, out_shape=tuple((jax.ShapeDtypeStruct(s, F32) f...  2.38 us

profile of v5, /device:TPU:1, one launch (start us, length us, event | category | flops | bytes accessed | tf_op | source)
XLA Modules:
  0.0 90.8 jit_solution(1999795567044478775)
XLA Ops:
  0.6 87.8 %shard_map.145 = (f32[48,96]{1,0:T(8,128)}, f32[49,96]{1,0:T(8,128)}, f32[96,384]{1,0:T(8,128)}, f32[96,384]{1,0:T(8,128)}, f32[192,384]{1,0:T(8,128)}, /*index=5*/f32[1,1,192,768]{3,2,1,0:T(8,128)}) custom-call(bf16[3,128,256]{2,1,0:T(8,128)(2,1)} %pix.1, bf16[48,96]{1,0:T(8,128)(2,1)} %ws.1, f32[49,96]{1,0:T(8,128)} %bitcast.9, bf16[96,384]{1,0:T(8,128)(2,1)} %we.1, ...), custom_call_target="tpu_custom_call" | custom-call | tf_op jit(solution)/shard_map/pallas_call | solution.py:622
  88.5 2.4 %shard_map.146 = (f32[48,96]{1,0:T(8,128)}, f32[49,96]{1,0:T(8,128)}, f32[96,384]{1,0:T(8,128)}, f32[96,384]{1,0:T(8,128)}, f32[192,384]{1,0:T(8,128)}, /*index=5*/f32[1,1,192,768]{3,2,1,0:T(8,128)}) custom-call(f32[48,96]{1,0:T(8,128)} %get-tuple-element.18.refs_0_, f32[49,96]{1,0:T(8,128)} %get-tuple-element.19.refs_1_, ...), custom_call_target="tpu_custom_call" | custom-call | tf_op jit(solution)/shard_map/pallas_call | solution.py:655
